TPU v7x, 32 devices: a whole 2x2x4 slice. The times are simulated.
32 devices in a mesh: wide: 8 (over z, x), narrow: 4 (over y, core).
Axes of the slice: x: 2, y: 2, z: 4, core: 2. Of those that a mesh axis runs over, the one named last changes fastest.
Arguments:
- tokens: bfloat16 [32768, 512], P(('wide', 'narrow')), may hold values from -6 to 6
- memory: bfloat16 [16384, 512], P(('wide', 'narrow')), may hold values from -6 to 6
- w_wide: bfloat16 [512, 6144], P(('wide', 'narrow'))
- w_tall: bfloat16 [3072, 512], P(('wide', 'narrow'))
- vecs: bfloat16 [512, 18], P(('wide', 'narrow'))
- avg_wide: float32 [512, 6144], P(('wide', 'narrow')), may hold values from -0.25 to 0.25
- avg_tall: float32 [3072, 512], P(('wide', 'narrow')), may hold values from -0.125 to 0.125
- avg_vecs: float32 [512, 18], P(('wide', 'narrow')), may hold values from -3 to 3
- tgt_lengths: int32 [32, 6], P(('wide', 'narrow')), may hold values from 1 to 512, 1024 in all within a row
- src_lengths: int32 [32, 6], P(('wide', 'narrow')), may hold values from 1 to 256, 512 in all within a row
- cotangent: bfloat16 [32768, 512], P(('wide', 'narrow')), may hold values from -6 to 6
Outputs:
- slots: bfloat16 [32768, 512], P(('wide', 'narrow'))
- grad_tokens: float32 [32768, 512], P(('wide', 'narrow'))
- grad_memory: float32 [16384, 512], P(('wide', 'narrow'))
- grad_wide: float32 [512, 6144], P(('wide', 'narrow'))
- grad_tall: float32 [3072, 512], P(('wide', 'narrow'))
- grad_vecs: float32 [512, 18], P(('wide', 'narrow'))
- new_avg_wide: float32 [512, 6144], P(('wide', 'narrow'))
- new_avg_tall: float32 [3072, 512], P(('wide', 'narrow'))
- new_avg_vecs: float32 [512, 18], P(('wide', 'narrow'))
Inputs may be any that keep to these rules, and one draw needn't show every extreme that they name: `tgt_lengths`: each row holds the 6 target segment lengths of one device's 1024 rows in order and sums to 1024; the last segment of every row is padding. `src_lengths`: each row holds the 6 source segment lengths of one device's 512 memory rows in order and sums to 512; target segment j reads source segment j.
All inputs are finite; a program needn't handle non-finite values.
Results may differ from a plain program's by a relative error of at most 0.019.
The roundings to bfloat16 on the way count: a program that leaves them out, or rounds other values in their place, can miss the bound.
Values may be sent and summed in bfloat16 or wider, within the bound.
A program may use at most 192 MiB of HBM per device.

v0:
```python
import jax
import jax.numpy as jnp
from jax import lax
from jax.sharding import PartitionSpec as P

D = 512
HEADS = 8
HEAD_DIM = 64
FF = 2048
SEGS = 6
AVG_STEPS = 4


SCORE_SCALE = 0.125
EPSILON = 1e-05
MASKED = -1e30


def matmul(left, right):
    return jnp.dot(left, right, preferred_element_type=jnp.float32)


def matmul_first(left, right):
    return lax.dot_general(
        left, right, (((0,), (0,)), ((), ())), preferred_element_type=jnp.float32
    )


def matmul_last(left, right):
    return lax.dot_general(
        left, right, (((1,), (1,)), ((), ())), preferred_element_type=jnp.float32
    )


def segment_numbers(lengths, count):
    endings = jnp.cumsum(lengths)
    places = jnp.arange(count, dtype=jnp.int32)
    return jnp.sum((places[:, None] >= endings[None, :]).astype(jnp.int32), axis=1)


def norm_forward(before, norm_gain, norm_shift):
    centred = before - jnp.mean(before, axis=-1, keepdims=True)
    inverse = lax.rsqrt(jnp.mean(centred * centred, axis=-1, keepdims=True) + EPSILON)
    normed = centred * inverse
    return (normed * norm_gain + norm_shift, normed, inverse)


def norm_backward(gradient, normed, inverse, norm_gain):
    scaled = gradient * norm_gain
    inner_sum = jnp.mean(scaled * normed, axis=-1, keepdims=True)
    before_grad = inverse * (scaled - jnp.mean(scaled, axis=-1, keepdims=True) - normed * inner_sum)
    return (before_grad, jnp.sum(gradient * normed, axis=0), jnp.sum(gradient, axis=0))


def split_heads(matrix):
    return matrix.reshape(matrix.shape[0], HEADS, HEAD_DIM)


def masked_scores(query_block, key_heads, segment_block, key_segment):
    scores = (
        jnp.einsum(
            "qhe,khe->hqk", split_heads(query_block), key_heads, preferred_element_type=jnp.float32
        )
        * SCORE_SCALE
    )
    allowed = segment_block[:, None] == key_segment[None, :]
    return jnp.where(allowed[None], scores, MASKED)


def attend_forward(queries, keys_in, values_in, query_segment, key_segment):
    row_count = queries.shape[0]
    block_rows = min(512, row_count)
    blocks = row_count // block_rows
    key_heads = split_heads(keys_in)
    value_heads = split_heads(values_in)

    def attend_block(pieces):
        query_block, segment_block = pieces
        scores = masked_scores(query_block, key_heads, segment_block, key_segment)
        highest = jnp.max(scores, axis=-1, keepdims=True)
        exponent = jnp.exp(scores - highest)
        totals = jnp.sum(exponent, axis=-1, keepdims=True)
        shares = (exponent / totals).astype(jnp.bfloat16)
        mixed = jnp.einsum("hqk,khe->qhe", shares, value_heads, preferred_element_type=jnp.float32)
        return (
            mixed.reshape(block_rows, HEADS * HEAD_DIM).astype(jnp.bfloat16),
            (highest + jnp.log(totals))[..., 0],
        )

    mixed, logsum = lax.map(
        attend_block,
        (queries.reshape(blocks, block_rows, -1), query_segment.reshape(blocks, block_rows)),
    )
    return (mixed.reshape(row_count, -1), logsum)


def attend_backward(queries, keys_in, values_in, mixed_grad, logsum, query_segment, key_segment):
    row_count = queries.shape[0]
    block_rows = min(512, row_count)
    blocks = row_count // block_rows
    key_heads = split_heads(keys_in)
    value_heads = split_heads(values_in)

    def backward_block(carried, pieces):
        key_sum, value_sum = carried
        query_block, grad_block, logsum_block, segment_block = pieces
        scores = masked_scores(query_block, key_heads, segment_block, key_segment)
        shares = jnp.exp(scores - logsum_block[..., None])
        grad_heads = split_heads(grad_block)
        share_grad = jnp.einsum(
            "qhe,khe->hqk", grad_heads, value_heads, preferred_element_type=jnp.float32
        )
        inner_sum = jnp.sum(shares * share_grad, axis=-1, keepdims=True)
        score_grad = (shares * (share_grad - inner_sum)).astype(jnp.bfloat16)
        query_grad = (
            jnp.einsum("hqk,khe->qhe", score_grad, key_heads, preferred_element_type=jnp.float32)
            * SCORE_SCALE
        )
        key_sum = (
            key_sum
            + jnp.einsum(
                "hqk,qhe->khe",
                score_grad,
                split_heads(query_block),
                preferred_element_type=jnp.float32,
            )
            * SCORE_SCALE
        )
        value_sum = value_sum + jnp.einsum(
            "hqk,qhe->khe",
            shares.astype(jnp.bfloat16),
            grad_heads,
            preferred_element_type=jnp.float32,
        )
        return ((key_sum, value_sum), query_grad.reshape(block_rows, HEADS * HEAD_DIM))

    zeros_init = jnp.zeros((keys_in.shape[0], HEADS, HEAD_DIM), jnp.float32)
    pieces = (
        queries.reshape(blocks, block_rows, -1),
        mixed_grad.reshape(blocks, block_rows, -1),
        logsum,
        query_segment.reshape(blocks, block_rows),
    )
    (key_sum, value_sum), query_grad = lax.scan(backward_block, (zeros_init, zeros_init), pieces)
    return (
        query_grad.reshape(row_count, -1),
        key_sum.reshape(keys_in.shape[0], -1),
        value_sum.reshape(values_in.shape[0], -1),
    )


def body(
    tokens,
    memory,
    w_wide,
    w_tall,
    vecs,
    avg_wide,
    avg_tall,
    avg_vecs,
    tgt_lengths,
    src_lengths,
    cotangent,
):
    wide_all, tall_all, vector_all = (
        lax.all_gather(w_wide, ("wide", "narrow"), axis=0, tiled=True),
        lax.all_gather(w_tall, ("wide", "narrow"), axis=0, tiled=True),
        lax.all_gather(vecs, ("wide", "narrow"), axis=0, tiled=True),
    )
    vectors = vector_all.astype(jnp.float32)
    spread = FF // D
    offset = 6 + spread
    columns = [wide_all[:, index * D : (index + 1) * D] for index in range(8)]
    target_query, target_key, target_value, target_output = (
        columns[0],
        columns[1],
        columns[2],
        columns[3],
    )
    source_query, source_key, source_value, source_output = (
        columns[4],
        columns[5],
        columns[6],
        columns[7],
    )
    up_weight = wide_all[:, 8 * D :]
    down_weight = tall_all[:FF]
    slot_left = tall_all[FF : FF + D]
    slot_right = tall_all[FF + D :]
    up_bias = vectors[:, 6:offset].T.reshape(FF)
    row_count = tokens.shape[0]
    target_segment = segment_numbers(tgt_lengths[0], row_count)
    source_segment = segment_numbers(src_lengths[0], memory.shape[0])
    valid_rows = (target_segment < SEGS - 1).astype(jnp.float32)[:, None]
    follow = (
        jnp.concatenate([target_segment[1:], jnp.full((1,), -1, jnp.int32)]) == target_segment
    ).astype(jnp.float32)[:, None]
    queries_self = (matmul(tokens, target_query) + vectors[:, 0]).astype(jnp.bfloat16)
    keys_self = matmul(tokens, target_key).astype(jnp.bfloat16)
    values_self = (matmul(tokens, target_value) + vectors[:, 1]).astype(jnp.bfloat16)
    mixed_self, logsum_self = attend_forward(
        queries_self, keys_self, values_self, target_segment, target_segment
    )
    first, normed_first, inverse_first = norm_forward(
        tokens.astype(jnp.float32) + matmul(mixed_self, target_output) + vectors[:, 2],
        vectors[:, offset + 2],
        vectors[:, offset + 3],
    )
    first_low = first.astype(jnp.bfloat16)
    queries_cross = (matmul(first_low, source_query) + vectors[:, 3]).astype(jnp.bfloat16)
    keys_cross = matmul(memory, source_key).astype(jnp.bfloat16)
    values_cross = (matmul(memory, source_value) + vectors[:, 4]).astype(jnp.bfloat16)
    mixed_cross, logsum_cross = attend_forward(
        queries_cross, keys_cross, values_cross, target_segment, source_segment
    )
    second, normed_second, inverse_second = norm_forward(
        first + matmul(mixed_cross, source_output) + vectors[:, 5],
        vectors[:, offset + 4],
        vectors[:, offset + 5],
    )
    second_low = second.astype(jnp.bfloat16)
    hidden = matmul(second_low, up_weight) + up_bias
    active = jax.nn.gelu(hidden).astype(jnp.bfloat16)
    third, normed_third, inverse_third = norm_forward(
        second + matmul(active, down_weight) + vectors[:, offset],
        vectors[:, offset + 6],
        vectors[:, offset + 7],
    )
    third_low = third.astype(jnp.bfloat16)
    right_half = jnp.concatenate([third_low[1:], jnp.zeros((1, D), jnp.bfloat16)]) * follow.astype(
        jnp.bfloat16
    )
    slots = (
        (matmul(third_low, slot_left) + matmul(right_half, slot_right) + vectors[:, offset + 1])
        * valid_rows
    ).astype(jnp.bfloat16)
    seed_grad = cotangent * valid_rows.astype(jnp.bfloat16)
    grad_slot_bias = jnp.sum(seed_grad.astype(jnp.float32), axis=0)
    grad_left = matmul_first(third_low, seed_grad)
    grad_right = matmul_first(right_half, seed_grad)
    right_back = matmul_last(seed_grad, slot_right) * follow
    grad_third = matmul_last(seed_grad, slot_left) + jnp.concatenate(
        [jnp.zeros((1, D), jnp.float32), right_back[:-1]]
    )
    grad_pre_third, grad_gain_third, grad_shift_third = norm_backward(
        grad_third, normed_third, inverse_third, vectors[:, offset + 6]
    )
    pre_third_low = grad_pre_third.astype(jnp.bfloat16)
    grad_down = matmul_first(active, pre_third_low)
    grad_tall_all = jnp.concatenate([grad_down, grad_left, grad_right], axis=0)
    gelu_value, gelu_pull = jax.vjp(jax.nn.gelu, hidden)
    grad_hidden = gelu_pull(matmul_last(pre_third_low, down_weight))[0]
    hidden_low = grad_hidden.astype(jnp.bfloat16)
    grad_up = matmul_first(second_low, hidden_low)
    grad_second = grad_pre_third + matmul_last(hidden_low, up_weight)
    grad_pre_second, grad_gain_second, grad_shift_second = norm_backward(
        grad_second, normed_second, inverse_second, vectors[:, offset + 4]
    )
    pre_second_low = grad_pre_second.astype(jnp.bfloat16)
    grad_source_output = matmul_first(mixed_cross, pre_second_low)
    mixed_cross_grad = matmul_last(pre_second_low, source_output).astype(jnp.bfloat16)
    cross_query_grad, cross_key_grad, cross_value_grad = attend_backward(
        queries_cross,
        keys_cross,
        values_cross,
        mixed_cross_grad,
        logsum_cross,
        target_segment,
        source_segment,
    )
    cross_query_low = cross_query_grad.astype(jnp.bfloat16)
    cross_key_low = cross_key_grad.astype(jnp.bfloat16)
    cross_value_low = cross_value_grad.astype(jnp.bfloat16)
    grad_source_query = matmul_first(first_low, cross_query_low)
    grad_source_key = matmul_first(memory, cross_key_low)
    grad_source_value = matmul_first(memory, cross_value_low)
    grad_memory = matmul_last(cross_key_low, source_key) + matmul_last(
        cross_value_low, source_value
    )
    grad_first = grad_pre_second + matmul_last(cross_query_low, source_query)
    grad_pre_first, grad_gain_first, grad_shift_first = norm_backward(
        grad_first, normed_first, inverse_first, vectors[:, offset + 2]
    )
    pre_first_low = grad_pre_first.astype(jnp.bfloat16)
    grad_target_output = matmul_first(mixed_self, pre_first_low)
    mixed_self_grad = matmul_last(pre_first_low, target_output).astype(jnp.bfloat16)
    self_query_grad, self_key_grad, self_value_grad = attend_backward(
        queries_self,
        keys_self,
        values_self,
        mixed_self_grad,
        logsum_self,
        target_segment,
        target_segment,
    )
    self_query_low = self_query_grad.astype(jnp.bfloat16)
    self_key_low = self_key_grad.astype(jnp.bfloat16)
    self_value_low = self_value_grad.astype(jnp.bfloat16)
    grad_target_query = matmul_first(tokens, self_query_low)
    grad_target_key = matmul_first(tokens, self_key_low)
    grad_target_value = matmul_first(tokens, self_value_low)
    grad_tokens = (
        grad_pre_first
        + matmul_last(self_query_low, target_query)
        + matmul_last(self_key_low, target_key)
        + matmul_last(self_value_low, target_value)
    )
    grad_wide_all = jnp.concatenate(
        [
            grad_target_query,
            grad_target_key,
            grad_target_value,
            grad_target_output,
            grad_source_query,
            grad_source_key,
            grad_source_value,
            grad_source_output,
            grad_up,
        ],
        axis=1,
    )
    bias_front = jnp.stack(
        [
            jnp.sum(self_query_grad, axis=0),
            jnp.sum(self_value_grad, axis=0),
            jnp.sum(grad_pre_first, axis=0),
            jnp.sum(cross_query_grad, axis=0),
            jnp.sum(cross_value_grad, axis=0),
            jnp.sum(grad_pre_second, axis=0),
        ],
        axis=1,
    )
    bias_middle = jnp.sum(grad_hidden, axis=0).reshape(spread, D).T
    bias_back = jnp.stack(
        [
            jnp.sum(grad_pre_third, axis=0),
            grad_slot_bias,
            grad_gain_first,
            grad_shift_first,
            grad_gain_second,
            grad_shift_second,
            grad_gain_third,
            grad_shift_third,
        ],
        axis=1,
    )
    grad_vector_all = jnp.concatenate([bias_front, bias_middle, bias_back], axis=1)
    grad_wide, grad_tall, grad_vecs = (
        lax.psum_scatter(grad_wide_all, ("wide", "narrow"), scatter_dimension=0, tiled=True),
        lax.psum_scatter(grad_tall_all, ("wide", "narrow"), scatter_dimension=0, tiled=True),
        lax.psum_scatter(grad_vector_all, ("wide", "narrow"), scatter_dimension=0, tiled=True),
    )
    new_avg_wide = avg_wide + (w_wide.astype(jnp.float32) - avg_wide) / AVG_STEPS
    new_avg_tall = avg_tall + (w_tall.astype(jnp.float32) - avg_tall) / AVG_STEPS
    new_avg_vecs = avg_vecs + (vecs.astype(jnp.float32) - avg_vecs) / AVG_STEPS
    return (
        slots,
        grad_tokens,
        grad_memory,
        grad_wide,
        grad_tall,
        grad_vecs,
        new_avg_wide,
        new_avg_tall,
        new_avg_vecs,
    )


def solution(mesh):
    in_specs = (
        P(("wide", "narrow"), None),
        P(("wide", "narrow"), None),
        P(("wide", "narrow"), None),
        P(("wide", "narrow"), None),
        P(("wide", "narrow"), None),
        P(("wide", "narrow"), None),
        P(("wide", "narrow"), None),
        P(("wide", "narrow"), None),
        P(("wide", "narrow"), None),
        P(("wide", "narrow"), None),
        P(("wide", "narrow"), None),
    )
    out_specs = (
        P(("wide", "narrow"), None),
        P(("wide", "narrow"), None),
        P(("wide", "narrow"), None),
        P(("wide", "narrow"), None),
        P(("wide", "narrow"), None),
        P(("wide", "narrow"), None),
        P(("wide", "narrow"), None),
        P(("wide", "narrow"), None),
        P(("wide", "narrow"), None),
    )
    return jax.shard_map(body, mesh=mesh, in_specs=in_specs, out_specs=out_specs, check_vma=False)
```

profile of v0, /device:TPU:0, one launch (start us, length us, event | category | flops | bytes accessed | tf_op | source)
XLA Modules:
  0.0 837.2 jit_solution(15932189220479719324)
XLA Ops:
  10.6 43.8 %all_gather.10 = bf16[512,18]{1,0:T(8,128)(2,1)S(1)} all-gather(bf16[16,18]{1,0:T(8,128)(2,1)} %param.23), channel_id=1, replica_groups=mesh['wide'=8,'narrow'=4] {'wide','narrow'}, dimensions={0}, use_global_device_ids=true | all-gather | bytes 19008 | tf_op jit(solution)/shard_map/all_gather | solution.py:168
  62.4 10.3 %all-gather.5.cloned.1.call-done = bf16[3072,512]{1,0:T(8,128)(2,1)} async-done(((bf16[96,512]{1,0:T(8,128)(2,1)}), bf16[3072,512]{1,0:T(8,128)(2,1)}) %all-gather.5.cloned.1.call-update) | async-done | bytes 3145744 | tf_op jit(solution)/shard_map/all_gather | solution.py:167
  76.2 67.9 %all-gather.3.cloned.1.call-done = bf16[512,6144]{1,0:T(8,128)(2,1)} async-done(((bf16[16,6144]{1,0:T(8,128)(2,1)}), bf16[512,6144]{1,0:T(8,128)(2,1)}) %all-gather.3.cloned.1.call-update) | async-done | bytes 6291472 | tf_op jit(solution)/shard_map/all_gather | solution.py:166
  152.7 34.6 %while.54 = (s32[]{:T(128)}, bf16[2,512,512]{2,1,0:T(8,128)(2,1)}, f32[2,8,512]{2,1,0:T(8,128)}, s32[2,512]{1,0:T(2,128)S(1)}, s32[1024]{0:T(1024)S(1)}, /*index...) while((s32[]{:T(128)}, bf16[2,512,512]{2,1,0:T(8,128)(2,1)}, ...), condition=%wide.region_5.6_spmd, body=%wide.region_2.0_spmd.sunk | while | flops 1124855808 | bytes 58861684 | solution.py:90
  161.4 5.8 fusion.215
  178.7 5.8 fusion.215
  198.9 16.7 %while.55 = (s32[]{:T(128)}, bf16[2,512,512]{2,1,0:T(8,128)(2,1)}, f32[2,8,512]{2,1,0:T(8,128)S(1)}, s32[2,512]{1,0:T(2,128)S(1)}, s32[512]{0:T(512)S(1)}, /*ind...) while((s32[]{:T(128)}, bf16[2,512,512]{2,1,0:T(8,128)(2,1)}, ...), condition=%wide.region_13.14_spmd, body=%wide.region_10.13_spmd.sunk | while | flops 562556928 | bytes 31596660 | solution.py:90
  219.2 4.6 fusion.45
  235.9 5.7 fusion.66
  241.6 9.2 %fusion.117 = (f32[2048]{0:T(1024)S(1)}, bf16[1024,2048]{1,0:T(8,128)(2,1)}) fusion(f32[1024,2048]{1,0:T(8,128)S(1)} %fusion.45, f32[2048]{0:T(1024)S(1)} %bitcast.289, bf16[3072,512]{1,0:T(8,128)(2,1)S(1)} %copy-done.57, f32[1024,512]{0,1:T(8,128)S(1)} %get-tuple-element.586), kind=kOutput, calls=%fused_computation.232 | convolution fusion | flops 2194143232 | bytes 16793600 | tf_op jit(solution)/shard_map/dot_general | solution.py:30
  251.4 7.7 multiply_reduce_fusion.3
  266.3 34.4 %while.56 = (s32[]{:T(128)}, f32[512,8,64]{0,2,1:T(8,128)}, f32[512,8,64]{0,2,1:T(8,128)}, f32[2,512,512]{1,2,0:T(8,128)}, bf16[2,512,512]{1,2,0:T(8,128)(2,1)S(...) while((s32[]{:T(128)}, f32[512,8,64]{0,2,1:T(8,128)}, ...), condition=%wide.region_24.25_spmd.clone, body=%wide.region_22.24_spmd.clone.sunk | while | flops 1375465472 | bytes 111796552 | solution.py:144
  320.2 94.0 %while.57 = (s32[]{:T(128)}, f32[1024,8,64]{0,2,1:T(8,128)}, f32[1024,8,64]{0,2,1:T(8,128)}, f32[2,512,512]{1,2,0:T(8,128)}, bf16[2,512,512]{1,2,0:T(8,128)(2,1)...) while((s32[]{:T(128)}, f32[1024,8,64]{0,2,1:T(8,128)}, ...), condition=%wide.region_29.30_spmd.clone, body=%wide.region_27.29_spmd.clone.sunk | while | flops 2725507072 | bytes 220293488 | solution.py:144
  329.9 11.8 %multiply_reduce_fusion.17 = (f32[8,512]{1,0:T(8,128)}, f32[8,512,1024]{2,1,0:T(8,128)}) fusion(f32[8,512,1024]{2,1,0:T(8,128)S(1)} %fusion.245, f32[8,512]{1,0:T(8,128)} %dynamic-slice_bitcast_fusion.5, bf16[512,8,64]{0,2,1:T(8,128)(2,1)} %bitcast.244, bf16[1024,8,64]{0,2,1:T(8,128)(2,1)} %get-tuple-element.999, ...), kind=kOutput, calls=%fused_computation.49.clone.1 | convolution fusion | flops 557838336 | bytes 35684352 | tf_op jit(solution)/shard_map/while/body/eval_jaxpr/qhe,khe->hqk/dot_general | solution.py:61
  341.7 9.3 %multiply_convert_fusion.9 = bf16[8,512,1024]{2,1,0:T(8,128)(2,1)} fusion(f32[8,512,1024]{2,1,0:T(8,128)} %get-tuple-element.871, f32[8,512,1024]{2,1,0:T(8,128)S(1)} %fusion.245, f32[8,512]{1,0:T(8,128)} %get-tuple-element.872), kind=kLoop, calls=%fused_computation.48.clone.1 | loop fusion | flops 12582912 | bytes 41959424 | tf_op jit(solution)/shard_map/while/body/eval_jaxpr/convert_element_type | solution.py:114
  351.0 8.9 %bitcast_add_fusion.5 = f32[1024,8,64]{0,2,1:T(8,128)} fusion(f32[1024,8,64]{0,2,1:T(8,128)} %get-tuple-element.981, bf16[512,8,64]{0,2,1:T(8,128)(2,1)S(1)} %bitcast.243, f32[8,512,1024]{2,1,0:T(8,128)} %get-tuple-element.871, pred[]{:T(512)S(6)} %compare.9), kind=kOutput, calls=%fused_computation.53.clone.1 | convolution fusion | flops 542113792 | bytes 21495808 | tf_op jit(solution)/shard_map/while/body/eval_jaxpr/hqk,qhe->khe/dot_general | solution.py:129
  376.4 11.8 %multiply_reduce_fusion.17 = (f32[8,512]{1,0:T(8,128)}, f32[8,512,1024]{2,1,0:T(8,128)}) fusion(f32[8,512,1024]{2,1,0:T(8,128)S(1)} %fusion.245, f32[8,512]{1,0:T(8,128)} %dynamic-slice_bitcast_fusion.5, bf16[512,8,64]{0,2,1:T(8,128)(2,1)} %bitcast.244, bf16[1024,8,64]{0,2,1:T(8,128)(2,1)} %get-tuple-element.999, ...), kind=kOutput, calls=%fused_computation.49.clone.1 | convolution fusion | flops 557838336 | bytes 35684352 | tf_op jit(solution)/shard_map/while/body/eval_jaxpr/qhe,khe->hqk/dot_general | solution.py:61
  388.2 9.3 %multiply_convert_fusion.9 = bf16[8,512,1024]{2,1,0:T(8,128)(2,1)} fusion(f32[8,512,1024]{2,1,0:T(8,128)} %get-tuple-element.871, f32[8,512,1024]{2,1,0:T(8,128)S(1)} %fusion.245, f32[8,512]{1,0:T(8,128)} %get-tuple-element.872), kind=kLoop, calls=%fused_computation.48.clone.1 | loop fusion | flops 12582912 | bytes 41959424 | tf_op jit(solution)/shard_map/while/body/eval_jaxpr/convert_element_type | solution.py:114
  397.5 9.5 %bitcast_add_fusion.5 = f32[1024,8,64]{0,2,1:T(8,128)} fusion(f32[1024,8,64]{0,2,1:T(8,128)} %get-tuple-element.981, bf16[512,8,64]{0,2,1:T(8,128)(2,1)S(1)} %bitcast.243, f32[8,512,1024]{2,1,0:T(8,128)} %get-tuple-element.871, pred[]{:T(512)S(6)} %compare.9), kind=kOutput, calls=%fused_computation.53.clone.1 | convolution fusion | flops 542113792 | bytes 21495808 | tf_op jit(solution)/shard_map/while/body/eval_jaxpr/hqk,qhe->khe/dot_general | solution.py:129
  422.0 5.5 pad_maximum_fusion
  467.5 4.5 convolution_dynamic-update-slice_fusion
  495.7 56.1 %reduce-scatter.10.cloned.1.call-done = f32[16,18]{1,0:T(8,128)} async-done(((f32[512,18]{1,0:T(8,128)}), f32[16,18]{1,0:T(8,128)}) %reduce-scatter.10.cloned.1.call-update) | async-done | bytes 1168
  551.9 117.5 %reduce-scatter.8.cloned.1.call-done = f32[96,512]{1,0:T(8,128)} async-done(((f32[3072,512]{1,0:T(8,128)}), f32[96,512]{1,0:T(8,128)}) %reduce-scatter.8.cloned.1.call-update) | async-done | bytes 196624 | tf_op jit(solution)/shard_map/reduce_scatter | solution.py:350
  669.4 161.1 %reduce-scatter.6.cloned.1.call-done = f32[16,6144]{1,0:T(8,128)} async-done(((f32[512,6144]{1,0:T(8,128)}), f32[16,6144]{1,0:T(8,128)}) %reduce-scatter.6.cloned.1.call-update) | async-done | bytes 393232 | tf_op jit(solution)/shard_map/reduce_scatter | solution.py:349
  (435 shorter events, 254.1 us)
Async XLA Ops:
  7.2 186.8 %copy-start = (bf16[512,512]{1,0:T(8,128)(2,1)S(1)}, bf16[512,512]{1,0:T(8,128)(2,1)}, u32[]{:S(2)}) copy-start(bf16[512,512]{1,0:T(8,128)(2,1)} %param.20) | copy-start | bytes 1572868
  7.2 65.5 %all-gather.5.cloned.1.call-start = ((), (), s32[]{:S(2)}) async-start(), calls=%async_computation.4 | async-start | bytes 3244032 | tf_op jit(solution)/shard_map/all_gather | solution.py:167
  7.9 136.1 %all-gather.3.cloned.1.call-start = ((), (), s32[]{:S(2)}) async-start(), calls=%async_computation.3 | async-start | bytes 6488064 | tf_op jit(solution)/shard_map/all_gather | solution.py:166
  8.7 543.2 %reduce-scatter.10.cloned.1.call-start = ((), (), s32[]{:S(2)}) async-start(), calls=%async_computation.7 | async-start | bytes 270336
  61.5 14.6 %copy-start.68 = (bf16[1024]{0:T(1024)(128)(2,1)}, bf16[1024]{0:T(1024)(128)(2,1)S(1)}, u32[]{:S(2)}) copy-start(bf16[1024]{0:T(1024)(128)(2,1)S(1)} %get-tuple-element.606) | copy-start | bytes 6148
  62.4 81.6 %copy-start.50 = (bf16[1024,512]{1,0:T(8,128)(2,1)S(1)}, bf16[1024,512]{1,0:T(8,128)(2,1)}, u32[]{:S(2)}) copy-start(bf16[1024,512]{1,0:T(8,128)(2,1)} %param.19) | copy-start | bytes 3145732
  152.7 34.7 %copy-start.101 = (f32[512]{0:T(512)S(1)}, f32[512]{0:T(512)}, u32[]{:S(2)}) copy-start(f32[512]{0:T(512)} %get-tuple-element.506) | copy-start | bytes 6148
  190.7 25.0 %copy-start.59 = (f32[1024]{0:T(1024)}, f32[1024]{0:T(1024)S(1)}, u32[]{:S(2)}) copy-start(f32[1024]{0:T(1024)S(1)} %broadcast_multiply_fusion.8) | copy-start | bytes 12292
  191.0 24.6 %copy-start.62 = (f32[1024]{0:T(1024)}, f32[1024]{0:T(1024)S(1)}, u32[]{:S(2)}) copy-start(f32[1024]{0:T(1024)S(1)} %add_rsqrt_fusion.2) | copy-start | bytes 12292
  198.9 16.7 %copy-start.98 = (f32[512]{0:T(512)S(1)}, f32[512]{0:T(512)}, u32[]{:S(2)}) copy-start(f32[512]{0:T(512)} %get-tuple-element.501) | copy-start | bytes 6148
  218.8 40.4 %copy-start.65 = (f32[1024]{0:T(1024)}, f32[1024]{0:T(1024)S(1)}, u32[]{:S(2)}) copy-start(f32[1024]{0:T(1024)S(1)} %broadcast_multiply_fusion.7) | copy-start | bytes 12292
  219.1 40.1 %copy-start.75 = (f32[1024]{0:T(1024)}, f32[1024]{0:T(1024)S(1)}, u32[]{:S(2)}) copy-start(f32[1024]{0:T(1024)S(1)} %add_rsqrt_fusion.1) | copy-start | bytes 12292
  232.1 9.5 %copy-start.25 = (bf16[1024,512]{0,1:T(8,128)(2,1)}, bf16[1024,512]{0,1:T(8,128)(2,1)S(1)}, u32[]{:S(2)}) copy-start(bf16[1024,512]{0,1:T(8,128)(2,1)S(1)} %get-tuple-element.601) | copy-start | bytes 3145732
  232.1 9.5 %copy-start.46 = (f32[1024,512]{0,1:T(8,128)}, f32[1024,512]{0,1:T(8,128)S(1)}, u32[]{:S(2)}) copy-start(f32[1024,512]{0,1:T(8,128)S(1)} %get-tuple-element.586) | copy-start | bytes 6291460
  300.7 8.3 copy-start.15
  300.7 8.3 copy-start.60
  300.7 8.3 copy-start.63
  300.7 8.3 copy-start.72
  351.0 8.9 %copy-start.1 = (bf16[8,512,1024]{2,1,0:T(8,128)(2,1)S(1)}, bf16[8,512,1024]{2,1,0:T(8,128)(2,1)}, u32[]{:S(2)}) copy-start(bf16[8,512,1024]{2,1,0:T(8,128)(2,1)} %multiply_convert_fusion.9) | copy-start | bytes 25165828 | tf_op jit(solution)/shard_map/while
  351.0 8.9 %copy-start.3 = (bf16[1024,8,64]{0,2,1:T(8,128)(2,1)S(1)}, bf16[1024,8,64]{0,2,1:T(8,128)(2,1)}, u32[]{:S(2)}) copy-start(bf16[1024,8,64]{0,2,1:T(8,128)(2,1)} %get-tuple-element.999) | copy-start | bytes 3145732 | tf_op jit(solution)/shard_map/while
  397.5 9.5 %copy-start.1 = (bf16[8,512,1024]{2,1,0:T(8,128)(2,1)S(1)}, bf16[8,512,1024]{2,1,0:T(8,128)(2,1)}, u32[]{:S(2)}) copy-start(bf16[8,512,1024]{2,1,0:T(8,128)(2,1)} %multiply_convert_fusion.9) | copy-start | bytes 25165828 | tf_op jit(solution)/shard_map/while
  397.5 9.5 %copy-start.3 = (bf16[1024,8,64]{0,2,1:T(8,128)(2,1)S(1)}, bf16[1024,8,64]{0,2,1:T(8,128)(2,1)}, u32[]{:S(2)}) copy-start(bf16[1024,8,64]{0,2,1:T(8,128)(2,1)} %get-tuple-element.999) | copy-start | bytes 3145732 | tf_op jit(solution)/shard_map/while
  419.4 250.0 %reduce-scatter.8.cloned.1.call-start = ((), (), s32[]{:S(2)}) async-start(), calls=%async_computation.6 | async-start | bytes 6488064 | tf_op jit(solution)/shard_map/reduce_scatter | solution.py:350
  427.5 403.0 %reduce-scatter.6.cloned.1.call-start = ((), (), s32[]{:S(2)}) async-start(), calls=%async_computation.5 | async-start | bytes 12976128 | tf_op jit(solution)/shard_map/reduce_scatter | solution.py:349
  (102 other events, 353.9 us)
Sparse Core Ops, SparseCore 0:
  10.9 61.7 all-gather.4
  75.6 68.4 all-gather.2
  419.5 132.3 reduce-scatter.9
  558.9 110.5 reduce-scatter.7
  675.9 154.5 reduce-scatter.5
where the time goes:
time: 848 us; the launch traced here: 837 us
  waiting for transfers between devices  414 us (49%)
  matrix products  209 us (25%)
  local copies, waits for them, and re-layouts  81.1 us (10%)
  other arithmetic  71.9 us (8%)
  blocking collectives  43.8 us (5%)
  between operations  15 us (2%)
    reduce_scatter x1, waiting for transfers between devices, body(): lax.psum_scatter(grad_wide_all, ('wide', 'narrow'), scatter_dimension=0,...  161 us
    reduce_scatter x1, waiting for transfers between devices, body(): lax.psum_scatter(grad_tall_all, ('wide', 'narrow'), scatter_dimension=0,...  118 us
    all_gather x1, waiting for transfers between devices, body(): lax.all_gather(w_wide, ('wide', 'narrow'), axis=0, tiled=True)  67.9 us
    unnamed x6, waiting for transfers between devices  57.6 us
    all_gather x1, blocking collectives, body(): lax.all_gather(vecs, ('wide', 'narrow'), axis=0, tiled=True)  43.8 us
    dot_general x12, matrix products, matmul_last(): lax.dot_general(left, right, (((1,), (1,)), ((), ())), preferred_element_...  42 us
    dot_general x8, matrix products, masked_scores(): jnp.einsum('qhe,khe->hqk', split_heads(query_block), key_heads, preferred...  35.2 us
    dot_general x12, matrix products, matmul(): return jnp.dot(left, right, preferred_element_type=jnp.float32)  31.4 us
  transfers between devices with their start and end apart: 5, of which 5 were waited for; matrix products, arithmetic and copies ran while one was open for 10% of the time, Pallas kernels for 0%

commit v1 on v0

--- a/solution.py
+++ b/solution.py
@@ -1,6 +1,10 @@
+import types
+
 import jax
 import jax.numpy as jnp
 from jax import lax
+from jax.experimental import pallas as pl
+from jax.experimental.pallas import tpu as pltpu
 from jax.sharding import PartitionSpec as P
 
 D = 512
@@ -149,7 +153,7 @@
     )
 
 
-def body(
+def plain_body(
     tokens,
     memory,
     w_wide,
@@ -366,6 +370,1149 @@
     )
 
 
+BF16 = jnp.bfloat16
+F32 = jnp.float32
+AUG = 80
+BIG = 1e30
+TILE = 256
+MESH_IDS = pl.DeviceIdType.MESH
+BIAS_OUT, GAIN = 10, 12
+TALL_CUT = 3
+OUT_SEMAPHORES = 24
+PAIR = 6 * HEAD_DIM
+GATHER_STEPS = {
+    4: ((0, 0), (1, 0), (0, 1), (2, 0), (1, 1), (0, 2), (3, 0), (0, 3),),
+    5: ((2, 1),),
+    8: ((4, 0),),
+    10: ((1, 2),),
+    13: ((3, 1),),
+    14: ((1, 3),),
+    18: ((5, 0),),
+    20: ((2, 2),),
+    23: ((4, 1),),
+    24: ((2, 3), (6, 0),),
+    29: ((3, 2),),
+    31: ((7, 0),),
+    33: ((3, 3),),
+    34: ((5, 1),),
+    37: ((8, 0),),
+    42: ((4, 2),),
+    44: ((6, 1),),
+    46: ((4, 3),),
+    54: ((7, 1),),
+    69: ((5, 2),),
+    75: ((8, 1),),
+    79: ((5, 3),),
+    81: ((6, 2),),
+    83: ((7, 2), (6, 3),),
+    84: ((8, 2), (7, 3), (8, 3),),
+}
+SUM_STEPS = {
+    2: ((0, 0), (1, 0),),
+    3: ((2, 0),),
+    7: ((0, 1),),
+    8: ((3, 0),),
+    9: ((4, 0), (1, 1),),
+    10: ((5, 0), (2, 1),),
+    11: ((0, 2),),
+    12: ((3, 1),),
+    13: ((4, 1),),
+    14: ((0, 3),),
+    15: ((1, 2), (5, 1),),
+    16: ((2, 2),),
+    17: ((3, 2),),
+    19: ((4, 2),),
+    20: ((5, 2),),
+    21: ((1, 3),),
+    23: ((7, 0), (2, 3),),
+    24: ((6, 0), (3, 3),),
+    25: ((4, 3), (7, 1),),
+    26: ((5, 3), (8, 0),),
+    27: ((6, 1), (7, 2),),
+    28: ((9, 0), (8, 1),),
+    29: ((6, 2), (10, 0),),
+    30: ((7, 3), (9, 1),),
+    31: ((8, 2), (10, 1),),
+    33: ((6, 3), (11, 0),),
+    34: ((9, 2),),
+    36: ((10, 2), (8, 3), (11, 1), (9, 3), (10, 3), (11, 2), (11, 3),),
+}
+
+
+def dot(left, right, left_dim, right_dim):
+    return lax.dot_general(
+        left, right, (((left_dim,), (right_dim,)), ((), ())), preferred_element_type=F32
+    )
+
+
+def bands(query_rows, key_rows, longest):
+    found = []
+    for start in range(0, query_rows, TILE):
+        if longest is None:
+            found.append((0, key_rows))
+            continue
+        low = max(0, (start - longest + 1) // TILE * TILE)
+        high = min(key_rows, -(-(start + TILE + longest - 1) // TILE) * TILE)
+        found.append((low, high))
+    return found
+
+
+def column_max(scores):
+    rows, columns = scores.shape
+    return jnp.max(
+        jnp.max(scores.reshape(rows // 64, 64, columns), axis=0), axis=0, keepdims=True
+    )
+
+
+def split_three(value):
+    high = value.astype(BF16).astype(F32)
+    middle = (value - high).astype(BF16).astype(F32)
+    low = (value - high - middle).astype(BF16).astype(F32)
+    return high, middle, low
+
+
+def feature_rows(base, first, parts):
+    place = lax.broadcasted_iota(jnp.int32, base.shape, 0)
+    for step, part in enumerate(parts):
+        base = jnp.where(place == first + step, part, base)
+    return base
+
+
+def gelu_pair(u):
+    scale = 0.7978845608028654
+    inner = jnp.tanh(scale * (u + 0.044715 * (u * u * u)))
+    half = 0.5 * (1.0 + inner)
+    slope = half + 0.5 * u * (1.0 - inner * inner) * (scale * (1.0 + 3 * 0.044715 * (u * u)))
+    return u * half, slope
+
+
+def normalize(before, gain, shift):
+    centred = before - jnp.mean(before, axis=-1, keepdims=True)
+    inverse = lax.rsqrt(jnp.mean(centred * centred, axis=-1, keepdims=True) + EPSILON)
+    normed = centred * inverse
+    return normed * gain + shift, normed, inverse
+
+
+def attention_forward(queries, keys, values, mixed, scores, ranges, heads, hooks):
+    tiles = len(ranges)
+
+    def put(head, tile):
+        low, high = ranges[tile]
+        scores[tile % 2][0 : high - low, :] = dot(
+            keys[head, :, low:high], queries[head, :, tile * TILE : (tile + 1) * TILE], 0, 0
+        )
+
+    put(heads[0], 0)
+
+    def one_head(head, carried):
+        for tile, (low, high) in enumerate(ranges):
+            if tile + 1 < tiles:
+                put(head, tile + 1)
+            else:
+                put(jnp.minimum(head + 1, heads[1] - 1), 0)
+            span = slice(tile * TILE, (tile + 1) * TILE)
+            current = scores[tile % 2][0 : high - low, :]
+            highest = column_max(current)
+            shares = jnp.exp(current - highest).astype(BF16)
+            gathered = dot(values[head, :, low:high], shares, 1, 0)
+            total = gathered[HEAD_DIM : HEAD_DIM + 1]
+            rows = pl.ds(pl.multiple_of(head * HEAD_DIM, HEAD_DIM), HEAD_DIM)
+            mixed[rows, span] = (gathered[:HEAD_DIM] * (1.0 / total)).astype(BF16)
+            queries[head, HEAD_DIM:, span] = feature_rows(
+                queries[head, HEAD_DIM:, span].astype(F32),
+                SEGS,
+                split_three(-(highest + jnp.log(total))),
+            ).astype(BF16)
+            for at, hook in hooks.items():
+                if at[1] == tile:
+                    pl.when(head == at[0])(hook)
+        return carried
+
+    lax.fori_loop(heads[0], heads[1], one_head, 0)
+
+
+def attention_backward(queries, keys, values, grads, outs, sums, shares, score_grads, ranges, hooks):
+    key_rows = keys.shape[2]
+    key_sum, value_sum = sums
+    tiles = len(ranges)
+
+    def put(head, tile):
+        low, high = ranges[tile]
+        span = slice(tile * TILE, (tile + 1) * TILE)
+        share = jnp.exp(dot(keys[head, :, low:high], queries[head, :, span], 0, 0))
+        share_grad = dot(values[head, :, low:high], grads[head, :, span], 0, 0)
+        shares[tile % 2][0 : high - low, :] = share.astype(BF16)
+        score_grads[tile % 2][0 : high - low, :] = (share * share_grad).astype(BF16)
+
+    put(0, 0)
+
+    def one_head(head, carried):
+        key_sum[:, 0:key_rows] = jnp.zeros((HEAD_DIM, key_rows), F32)
+        value_sum[:, 0:key_rows] = jnp.zeros((HEAD_DIM, key_rows), F32)
+        query_out, key_out, value_out = [out(head) for out in outs]
+        for tile, (low, high) in enumerate(ranges):
+            if tile + 1 < tiles:
+                put(head, tile + 1)
+            else:
+                put(jnp.minimum(head + 1, HEADS - 1), 0)
+            span = slice(tile * TILE, (tile + 1) * TILE)
+            share = shares[tile % 2][0 : high - low, :]
+            score_grad = score_grads[tile % 2][0 : high - low, :]
+            query_out[:, span] = (
+                dot(keys[head, 0:HEAD_DIM, low:high], score_grad, 1, 0) * SCORE_SCALE
+            ).astype(BF16)
+            key_sum[:, low:high] += dot(queries[head, 0:HEAD_DIM, span], score_grad, 1, 1)
+            value_sum[:, low:high] += dot(grads[head, 0:HEAD_DIM, span], share, 1, 1)
+        key_out[...] = key_sum[:, 0:key_rows].astype(BF16)
+        value_out[...] = value_sum[:, 0:key_rows].astype(BF16)
+        for at, hook in hooks.items():
+            pl.when(head == at)(hook)
+        return carried
+
+    lax.fori_loop(0, HEADS, one_head, 0)
+
+
+class Exchange:
+    def __init__(self, wide, narrow):
+        self.narrow_bits = narrow.bit_length() - 1
+        self.count = (wide * narrow).bit_length() - 1
+        self.line = 1 << (self.count - 3)
+        self.place = (lax.axis_index("wide"), lax.axis_index("narrow"))
+        number = self.place[0] * narrow + self.place[1]
+        self.bits = [(number >> bit) & 1 for bit in range(self.count)]
+        self.own = tuple(self.bits[bit] for bit in reversed(range(self.count)))
+        self.far = list(range(3, self.count))
+        self.masks = [1, 2, 4] + [other << 3 for other in range(1, self.line)]
+
+    def device(self, mask):
+        wide, narrow = self.place
+        return (wide ^ (mask >> self.narrow_bits), narrow ^ (mask & ((1 << self.narrow_bits) - 1)))
+
+    def greet(self):
+        barrier = pltpu.get_barrier_semaphore()
+        for mask in self.masks:
+            pl.semaphore_signal(
+                barrier, inc=1, device_id=self.device(mask), device_id_type=MESH_IDS
+            )
+
+    def meet(self):
+        pl.semaphore_wait(pltpu.get_barrier_semaphore(), len(self.masks))
+
+    def by_core(self, split, act):
+        if split:
+            pl.when(self.bits[0] == 0)(lambda: act((1, 2)))
+            pl.when(self.bits[0] == 1)(lambda: act((2, 1)))
+        else:
+            act((1, 2))
+
+    def view(self, part, open_bits, flipped=0):
+        index = tuple(
+            slice(None)
+            if bit in open_bits
+            else (1 - self.bits[bit] if flipped >> bit & 1 else self.bits[bit])
+            for bit in reversed(range(self.count))
+        )
+        return part.ref.at[index + part.where]
+
+
+class Part:
+    def __init__(self, ref, rows=None, columns=None, buffers=(), outs=()):
+        cut = lambda ends: slice(None) if ends is None else pl.ds(ends[0], ends[1] - ends[0])
+        self.ref, self.where, self.buffers, self.outs = ref, (cut(rows), cut(columns)), buffers, outs
+
+
+class Transfer:
+    def __init__(self, net, pieces, send, receive):
+        self.net, self.pieces, self.send, self.receive = net, pieces, send, receive
+
+    def copy(self, piece, part, slot, source, target, mask):
+        return pltpu.make_async_remote_copy(
+            source,
+            target,
+            self.send.at[piece, slot, part],
+            self.receive.at[piece, slot, part],
+            device_id=self.net.device(mask),
+            device_id_type=MESH_IDS,
+        )
+
+    def finish(self):
+        for piece in range(len(self.pieces)):
+            for stage in range(4):
+                self.each(piece, stage, lambda copy: copy.wait_send())
+
+
+class Gather(Transfer):
+    def each(self, piece, stage, act):
+        net = self.net
+
+        def with_order(near):
+            first, second = near
+            for number, part in enumerate(self.pieces[piece]):
+                if stage == 0:
+                    for other in range(1, net.line):
+                        view = net.view(part, [])
+                        act(self.copy(piece, number, other + 3, view, view, other << 3))
+                elif stage == 1:
+                    view = net.view(part, net.far)
+                    act(self.copy(piece, number, 0, view, view, 1 << first))
+                elif stage == 2:
+                    view = net.view(part, net.far)
+                    act(self.copy(piece, number, 1, view, view, 1 << second))
+                    view = net.view(part, net.far, 1 << first)
+                    act(self.copy(piece, number, 2, view, view, 1 << second))
+                else:
+                    view = net.view(part, net.far + [1, 2])
+                    act(self.copy(piece, number, 3, view, view, 1))
+
+        net.by_core(stage in (1, 2), with_order)
+
+    def start(self, piece):
+        if piece < len(self.pieces):
+            self.each(piece, 0, lambda copy: copy.start())
+
+    def step(self, piece, stage):
+        net = self.net
+        self.each(piece, stage, lambda copy: copy.wait_recv())
+        if stage == 0:
+            self.each(piece, 1, lambda copy: copy.start())
+            self.send_second(piece, 0)
+            self.start(piece + 2)
+        elif stage == 1:
+            self.send_second(piece, 1)
+        elif stage == 2:
+            self.each(piece, 3, lambda copy: copy.start())
+
+    def send_second(self, piece, which):
+        net = self.net
+
+        def with_order(near):
+            first, second = near
+            for number, part in enumerate(self.pieces[piece]):
+                view = net.view(part, net.far, which << first)
+                self.copy(piece, number, 1 + which, view, view, 1 << second).start()
+
+        net.by_core(True, with_order)
+
+
+class Sum(Transfer):
+    def each(self, piece, stage, act):
+        net = self.net
+
+        def with_order(near):
+            first, second = near
+            for number, part in enumerate(self.pieces[piece]):
+                arrive = part.buffers
+                if stage == 0:
+                    view = net.view(part, net.far + [1, 2], 1)
+                    act(self.copy(piece, number, 0, view, arrive[0], 1))
+                elif stage == 1:
+                    view = net.view(part, net.far, (1 << first) | (1 << second))
+                    act(self.copy(piece, number, 1, view, arrive[1], 1 << second))
+                elif stage == 2:
+                    view = net.view(part, net.far, 1 << second)
+                    act(self.copy(piece, number, 2, view, arrive[2], 1 << second))
+                    view = net.view(part, net.far, 1 << first)
+                    act(self.copy(piece, number, 3, view, arrive[3], 1 << first))
+                else:
+                    for other in range(1, net.line):
+                        view = net.view(part, [], other << 3)
+                        act(self.copy(piece, number, other + 3, view, arrive[4].at[other - 1], other << 3))
+
+        net.by_core(stage in (1, 2), with_order)
+
+    def send_one(self, piece, which):
+        net = self.net
+
+        def with_order(near):
+            bit = near[1 - which]
+            for number, part in enumerate(self.pieces[piece]):
+                view = net.view(part, net.far, 1 << bit)
+                self.copy(
+                    piece, number, 2 + which, view, part.buffers[2 + which], 1 << bit
+                ).start()
+
+        net.by_core(True, with_order)
+
+    def start(self, piece):
+        self.each(piece, 0, lambda copy: copy.start())
+
+    def add(self, piece, stage):
+        net = self.net
+
+        def with_order(near):
+            rest = sorted(net.far + ([1, 2] if stage == 0 else []))
+            flipped = near[0] if stage == 1 else None
+
+            def one_shard(step, carried):
+                place = {bit: (step >> at) & 1 for at, bit in enumerate(rest)}
+                index = tuple(
+                    place[bit]
+                    if bit in place
+                    else (1 - net.bits[bit] if bit == flipped else net.bits[bit])
+                    for bit in reversed(range(net.count))
+                )
+                arrived = tuple(place[bit] for bit in reversed(rest)) + (slice(None), slice(None))
+                for part in self.pieces[piece]:
+                    where = index + part.where
+                    value = part.ref[where].astype(F32)
+                    for buffer in part.buffers[2:4] if stage == 2 else part.buffers[stage : stage + 1]:
+                        value = value + buffer[arrived].astype(F32)
+                    part.ref[where] = value.astype(part.ref.dtype)
+                return carried
+
+            lax.fori_loop(0, 1 << len(rest), one_shard, 0)
+
+        if stage < 3:
+            net.by_core(stage == 1, with_order)
+            return
+        for part in self.pieces[piece]:
+            value = part.ref[net.own + part.where].astype(F32)
+            for other in range(1, net.line):
+                value = value + part.buffers[4][other - 1].astype(F32)
+            for low, high, staged, out, semaphore in part.outs:
+                staged[...] = value[:, low:high]
+                pltpu.make_async_copy(staged, out, semaphore).start()
+
+    def step(self, piece, stage):
+        self.each(piece, stage, lambda copy: copy.wait_recv())
+        self.add(piece, stage)
+        if stage == 0:
+            self.each(piece, 1, lambda copy: copy.start())
+            self.send_one(piece, 0)
+        elif stage == 1:
+            self.send_one(piece, 1)
+        elif stage == 2:
+            self.each(piece, 3, lambda copy: copy.start())
+
+    def finish(self):
+        super().finish()
+        for piece in self.pieces:
+            for part in piece:
+                for _, _, staged, out, semaphore in part.outs:
+                    pltpu.make_async_copy(staged, out, semaphore).wait()
+
+
+class Plan:
+    def __init__(self, transfer, table):
+        self.transfer, self.table, self.stop = transfer, table, 0
+
+    def next(self):
+        taken = self.table.get(self.stop, ())
+        self.stop += 1
+
+        def act():
+            for piece, stage in taken:
+                self.transfer.step(piece, stage)
+
+        return act if taken else None
+
+    def now(self):
+        act = self.next()
+        if act:
+            act()
+
+    def loop(self, places):
+        found = {place: self.next() for place in places}
+        return {place: act for place, act in found.items() if act}
+
+
+def layer_kernel(r, wide_size, narrow_size):
+    net = Exchange(wide_size, narrow_size)
+    net.greet()
+    devices = wide_size * narrow_size
+    wide7, tall7, vec7, gvec7 = r.wide, r.tall, r.vec, r.grad_vec
+    wide = wide7.reshape(devices * wide7.shape[-2], wide7.shape[-1])
+    tall = tall7.reshape(devices * tall7.shape[-2], tall7.shape[-1])
+    slope7 = r.slope
+    slope = slope7.reshape(devices * slope7.shape[-2], slope7.shape[-1])
+    own_rows = (0, wide7.shape[-2])
+    tokens, memory, seed, seed_next = r.tokens, r.memory, r.seed, r.seed_next
+    rows, sources = tokens.shape[0], memory.shape[0]
+    tiles = rows // TILE
+    local = r.local
+
+    wide_moves = [
+        (block * D + pair * PAIR // 3, pair * PAIR + block * PAIR // 3, PAIR // 3)
+        for pair in range(HEADS // 2)
+        for block in range(3)
+    ] + [(3 * D, 3 * D, wide7.shape[-1] - 3 * D)]
+    loads = [
+        pltpu.make_async_copy(
+            r.w_wide.at[:, pl.ds(low, width)],
+            wide7.at[net.own + (slice(None), pl.ds(high, width))],
+            r.own_done.at[number],
+        )
+        for number, (low, high, width) in enumerate(wide_moves)
+    ] + [
+        pltpu.make_async_copy(r.w_tall, tall7.at[net.own], local.at[1]),
+        pltpu.make_async_copy(r.vecs, vec7.at[net.own], local.at[2]),
+        pltpu.make_async_copy(r.tokens_in, tokens, local.at[3]),
+        pltpu.make_async_copy(r.memory_in, memory, local.at[4]),
+        pltpu.make_async_copy(r.cotangent, seed, local.at[5]),
+    ]
+    for copy in loads:
+        copy.start()
+
+    tall_rows = tall7.shape[-2]
+    tall_cuts = [(low, low + tall_rows // TALL_CUT) for low in range(0, tall_rows, tall_rows // TALL_CUT)]
+
+    def wide_part(low, high):
+        return [Part(wide7, None, (low, high))]
+
+    gather = Gather(
+        net,
+        [
+            wide_part(0, 2 * PAIR) + [Part(vec7)],
+            wide_part(2 * PAIR, 4 * PAIR),
+            wide_part(3 * D, 5 * D),
+            wide_part(5 * D, 7 * D),
+            wide_part(7 * D, 9 * D),
+            wide_part(9 * D, 12 * D),
+        ]
+        + [[Part(tall7, cut)] for cut in tall_cuts],
+        r.gather_send,
+        r.gather_receive,
+    )
+    plan = Plan(gather, GATHER_STEPS)
+    out_semaphores = iter(range(OUT_SEMAPHORES))
+
+    def out_of(low, high, staged, out):
+        return (low, high, staged, out, r.out_done.at[next(out_semaphores)])
+
+    def wide_out(low, high, start):
+        columns = pl.ds(start, high - low)
+        return out_of(low, high, r.out_wide.at[:, columns], r.grad_wide.at[:, columns])
+
+    def tall_sum(cut, buffers):
+        place = pl.ds(cut[0], cut[1] - cut[0])
+        out = out_of(0, D, r.out_tall.at[place, :], r.grad_tall.at[place, :])
+        return [Part(tall7, cut, None, buffers, [out])]
+
+    def wide_sum(low, high, buffers):
+        return [Part(wide7, None, (low, high), buffers, [wide_out(0, high - low, low)])]
+
+    def self_sum(pair):
+        third = PAIR // 3
+        outs = [
+            wide_out(block * third, (block + 1) * third, block * D + pair * third)
+            for block in range(3)
+        ]
+        buffers = [
+            buffer.at[
+                (slice(None),) * (len(buffer.shape) - 1) + (pl.ds(pair % 2 * PAIR, PAIR),)
+            ]
+            for buffer in r.in_wide[pair // 2]
+        ]
+        columns = (pair * PAIR, (pair + 1) * PAIR)
+        return [Part(slope7, own_rows, columns, buffers, outs)]
+
+    vec_sum = Part(gvec7, None, None, r.in_vec, [out_of(0, 128, r.out_vec, r.grad_vecs)])
+    ranges_of_sum = ((8, 10), (10, 12), (7, 8), (3, 5), (5, 7))
+    total = Sum(
+        net,
+        [tall_sum(cut, buffers) for cut, buffers in zip(tall_cuts, r.in_tall)]
+        + [
+            wide_sum(low * D, high * D, buffers)
+            for (low, high), buffers in zip(ranges_of_sum, r.in_wide)
+        ]
+        + [self_sum(pair) + ([vec_sum] if pair == HEADS // 2 - 1 else []) for pair in range(HEADS // 2)],
+        r.sum_send,
+        r.sum_receive,
+    )
+    TALL, UP, OUT2, MID, KEYS2, SELF = 0, TALL_CUT, TALL_CUT + 2, TALL_CUT + 3, TALL_CUT + 4, TALL_CUT + 5
+    sum_plan = Plan(total, SUM_STEPS)
+
+    for copy in loads[:-3]:
+        copy.wait()
+    net.meet()
+    gather.start(0)
+
+    def endings(lengths):
+        found, running = [], 0
+        for index in range(SEGS):
+            running = running + lengths[0, index]
+            found.append(running)
+        return found
+
+    target_ends = endings(r.tgt_lengths)
+    source_ends = endings(r.src_lengths)
+
+    def chosen(ends, count):
+        place = lax.broadcasted_iota(jnp.int32, (16, count), 1)
+        segment = jnp.zeros((16, count), jnp.int32)
+        for end in ends:
+            segment = segment + (place >= end).astype(jnp.int32)
+        return segment == lax.broadcasted_iota(jnp.int32, (16, count), 0)
+
+    def query_features(ends, count):
+        return jnp.where(chosen(ends, count), 1.0, 0.0).astype(BF16)
+
+    def key_features(ends, count):
+        row = lax.broadcasted_iota(jnp.int32, (16, count), 0)
+        masked = jnp.where(chosen(ends, count), 0.0, -BIG)
+        return jnp.where(row < SEGS, masked, jnp.where(row < SEGS + 3, 1.0, 0.0)).astype(BF16)
+
+    def value_features(count):
+        row = lax.broadcasted_iota(jnp.int32, (16, count), 0)
+        return jnp.where(row < 3, 1.0, 0.0).astype(BF16)
+
+    def every_head(ref, features):
+        ref[:, HEAD_DIM:, :] = jnp.broadcast_to(features[None], (HEADS,) + features.shape)
+
+    q, k, v, q2, k2, v2 = r.q, r.k, r.v, r.q2, r.k2, r.v2
+    every_head(q, query_features(target_ends, rows))
+    every_head(q2, query_features(target_ends, rows))
+    every_head(k, key_features(target_ends, rows))
+    every_head(k2, key_features(source_ends, sources))
+    gather.start(1)
+    plan.now()
+    every_head(v, value_features(rows))
+    every_head(v2, value_features(sources))
+    plan.now()
+
+    def position(tile):
+        return tile * TILE + lax.broadcasted_iota(jnp.int32, (TILE, 1), 0)
+
+    def valid(tile):
+        return jnp.where(position(tile) < target_ends[SEGS - 2], 1.0, 0.0)
+
+    def follow(tile):
+        after = position(tile) + 1
+        ended = after == target_ends[0]
+        for end in target_ends[1:]:
+            ended = ended | (after == end)
+        return jnp.where(ended, 0.0, 1.0)
+
+    def span(tile):
+        return pl.ds(tile * TILE, TILE)
+
+    shift, res = r.shift, r.res
+    loads[-1].wait()
+    shift[0:8, :] = jnp.zeros((8, D), F32)
+    for tile in range(tiles):
+        masked = seed[span(tile), :].astype(F32) * valid(tile)
+        seed[span(tile), :] = masked.astype(BF16)
+        shift[pl.ds(tile * TILE + 8, TILE), :] = masked * follow(tile)
+    plan.now()
+    for tile in range(tiles):
+        seed_next[span(tile), :] = shift[pl.ds(tile * TILE + 7, TILE), :].astype(BF16)
+    shift[rows : rows + 8, :] = jnp.zeros((8, D), F32)
+    r.grad_rows[...] = jnp.zeros_like(r.grad_rows)
+    r.grad_columns[...] = jnp.zeros_like(r.grad_columns)
+    loads[-3].wait()
+    loads[-2].wait()
+    plan.now()
+
+    def row(index):
+        return r.row_vectors[index : index + 1, :]
+
+    def column(index):
+        return vec7[...].reshape(D, vec7.shape[-1])[:, index : index + 1].astype(F32)
+
+    def heads_of(value):
+        return value.reshape(value.shape[0] // HEAD_DIM, HEAD_DIM, value.shape[1])
+
+    def scaled(value):
+        return (value.astype(BF16).astype(F32) * SCORE_SCALE).astype(BF16)
+
+    def wide_column(index):
+        return wide[:, index * D : (index + 1) * D]
+
+    self_ranges = bands(rows, rows, 512)
+    cross_ranges = bands(rows, sources, None)
+    a, a2 = r.mixed, r.mixed2
+    halves = [(index * HEADS // 2, (index + 1) * HEADS // 2) for index in range(2)]
+
+    bias_rows = PAIR // 3
+    identity = lax.broadcasted_iota(jnp.int32, (D, D), 0) == lax.broadcasted_iota(
+        jnp.int32, (D, D), 1
+    )
+    identity = jnp.where(identity, 1.0, 0.0).astype(BF16)
+    for index, heads in enumerate(halves):
+        plan.now()
+        if index == 0:
+            r.row_vectors[0 : vec7.shape[-1], :] = dot(
+                vec7[...].reshape(D, vec7.shape[-1]), identity, 0, 0
+            )
+        columns = slice(2 * index * PAIR, 2 * (index + 1) * PAIR)
+        biases = []
+        for pair in (2 * index, 2 * index + 1):
+            place = slice(pair * bias_rows, (pair + 1) * bias_rows)
+            biases += [column(0)[place], jnp.zeros((bias_rows, 1), F32), column(1)[place]]
+        bias = jnp.concatenate(biases, axis=0)
+        for tile in range(tiles):
+            both = (dot(wide[:, columns], tokens[span(tile), :], 0, 1) + bias).astype(BF16)
+            for pair in range(2):
+                group = slice(heads[0] + 2 * pair, heads[0] + 2 * pair + 2)
+                for block, ref in enumerate((q, k, v)):
+                    start = pair * PAIR + block * bias_rows
+                    value = both[start : start + bias_rows]
+                    if block == 0:
+                        value = (value.astype(F32) * SCORE_SCALE).astype(BF16)
+                    ref[group, 0:HEAD_DIM, span(tile)] = heads_of(value)
+        plan.now()
+        attention_forward(
+            q,
+            k,
+            v,
+            a,
+            r.scores,
+            self_ranges,
+            heads,
+            plan.loop([(head, tile) for head in range(*heads) for tile in range(tiles)]),
+        )
+
+    normed, low, inverse = r.normed, r.low, r.inverse
+
+    def norm_tile(index, tile, before):
+        out, unit, rho = normalize(before, row(GAIN + 2 * index), row(GAIN + 2 * index + 1))
+        normed[index][span(tile), :] = unit.astype(BF16)
+        inverse[span(tile), index : index + 1] = rho
+        low[index][span(tile), :] = out.astype(BF16)
+        return out
+
+    plan.now()
+    for tile in range(tiles):
+        before = (
+            tokens[span(tile), :].astype(F32) + dot(a[:, span(tile)], wide_column(3), 0, 0) + row(2)
+        )
+        out = norm_tile(0, tile, before)
+        res[span(tile), :] = out
+        q2[:, 0:HEAD_DIM, span(tile)] = heads_of(
+            scaled(dot(wide_column(4), out.astype(BF16), 0, 1) + column(3))
+        )
+        plan.now()
+    plan.now()
+    for tile in range(sources // TILE):
+        part = memory[span(tile), :]
+        k2[:, 0:HEAD_DIM, span(tile)] = heads_of(dot(wide_column(5), part, 0, 1).astype(BF16))
+        v2[:, 0:HEAD_DIM, span(tile)] = heads_of(
+            (dot(wide_column(6), part, 0, 1) + column(4)).astype(BF16)
+        )
+    attention_forward(
+        q2,
+        k2,
+        v2,
+        a2,
+        r.scores,
+        cross_ranges,
+        (0, HEADS),
+        plan.loop([(head, tile) for head in range(HEADS) for tile in range(tiles)]),
+    )
+    active = r.active
+    plan.now()
+    for tile in range(tiles):
+        before = res[span(tile), :] + dot(a2[:, span(tile)], wide_column(7), 0, 0) + row(5)
+        out = norm_tile(1, tile, before)
+        res[span(tile), :] = out
+        for block in range(FF // D):
+            if tile == 0 and block == 1:
+                plan.now()
+            columns = slice(block * D, (block + 1) * D)
+            u = dot(out.astype(BF16), wide_column(8 + block), 1, 0) + row(6 + block)
+            value, derivative = gelu_pair(u)
+            active[span(tile), columns] = value.astype(BF16)
+            slope[span(tile), columns] = derivative.astype(BF16)
+        plan.now()
+    plan.now()
+    slot_left = tall.at[pl.ds(FF, D), :]
+    slot_right = tall.at[pl.ds(FF + D, D), :]
+    for tile in range(tiles):
+        before = (
+            res[span(tile), :] + dot(active[span(tile), :], tall[0:FF, :], 1, 0) + row(BIAS_OUT)
+        )
+        out = norm_tile(2, tile, before).astype(BF16)
+        shift[span(tile), :] = dot(out, slot_right[...], 1, 0)
+    low_grad = r.low_grad
+    slot_copies = []
+    for tile in range(tiles):
+        low_grad[span(tile), :] = (
+            (
+                dot(low[2][span(tile), :], slot_left[...], 1, 0)
+                + follow(tile) * shift[pl.ds(tile * TILE + 1, TILE), :]
+                + row(BIAS_OUT + 1)
+            )
+            * valid(tile)
+        ).astype(BF16)
+        copy = pltpu.make_async_copy(
+            low_grad.at[span(tile), :], r.slots.at[span(tile), :], local.at[6 + tile]
+        )
+        copy.start()
+        slot_copies.append(copy)
+    gather.finish()
+
+    grad_rows, grad_columns = r.grad_rows, r.grad_columns
+
+    def add_row(index, value):
+        grad_rows[index : index + 1, :] += jnp.sum(value, axis=0, keepdims=True)
+
+    def norm_back(index, tile, gradient, bias_row):
+        gain = row(GAIN + 2 * index)
+        unit = normed[index][span(tile), :].astype(F32)
+        scaled_grad = gradient * gain
+        inner = jnp.mean(scaled_grad * unit, axis=-1, keepdims=True)
+        before = inverse[span(tile), index : index + 1] * (
+            scaled_grad - jnp.mean(scaled_grad, axis=-1, keepdims=True) - unit * inner
+        )
+        add_row(GAIN + 2 * index, gradient * unit)
+        add_row(GAIN + 2 * index + 1, gradient)
+        add_row(bias_row, before)
+        res[span(tile), :] = before
+        low_grad[span(tile), :] = before.astype(BF16)
+
+    for tile in range(tiles):
+        part = seed[span(tile), :]
+        add_row(BIAS_OUT + 1, part.astype(F32))
+        gradient = dot(part, slot_left[...], 1, 1) + dot(
+            seed_next[span(tile), :], slot_right[...], 1, 1
+        )
+        slot_copies[tile].wait()
+        norm_back(2, tile, gradient, BIAS_OUT)
+    slot_left[...] = dot(low[2][...], seed[...], 0, 0).astype(BF16)
+    slot_right[...] = dot(low[2][...], seed_next[...], 0, 0).astype(BF16)
+    for block in range(FF // D):
+        columns = slice(block * D, (block + 1) * D)
+        for tile in range(tiles):
+            grad = dot(low_grad[span(tile), :], tall[columns, :], 1, 1) * slope[
+                span(tile), columns
+            ].astype(F32)
+            add_row(6 + block, grad)
+            slope[span(tile), columns] = grad.astype(BF16)
+        tall[columns, :] = dot(active[:, columns], low_grad[...], 0, 0).astype(BF16)
+    for cut in range(TALL_CUT):
+        total.start(TALL + cut)
+    for tile in range(tiles):
+        gradient = res[span(tile), :] + dot(
+            slope[span(tile), :], wide[:, 8 * D : 8 * D + FF], 1, 1
+        )
+        norm_back(1, tile, gradient, 5)
+        sum_plan.now()
+    for block in range(FF // D):
+        columns = slice(block * D, (block + 1) * D)
+        wide[:, 8 * D + block * D : 8 * D + (block + 1) * D] = dot(
+            low[1][...], slope[:, columns], 0, 0
+        ).astype(BF16)
+        if block % 2 == 1:
+            total.start(UP + block // 2)
+        sum_plan.now()
+    grads = r.mixed_grad
+
+    def mixed_back(weight_index, mixed):
+        for tile in range(tiles):
+            grad = dot(wide_column(weight_index), low_grad[span(tile), :], 1, 1).astype(BF16)
+            grads[:, 0:HEAD_DIM, span(tile)] = heads_of(grad)
+            inner = jnp.sum(
+                heads_of(grad.astype(F32) * mixed[:, span(tile)].astype(F32)),
+                axis=1,
+                keepdims=True,
+            )
+            place = lax.broadcasted_iota(jnp.int32, (HEADS, 16, TILE), 1)
+            features = jnp.zeros((HEADS, 16, TILE), F32)
+            for step, part in enumerate(split_three(-inner)):
+                features = jnp.where(place == step, part, features)
+            grads[:, HEAD_DIM:, span(tile)] = features.astype(BF16)
+        wide[:, weight_index * D : (weight_index + 1) * D] = dot(
+            mixed[...], low_grad[...], 1, 0
+        ).astype(BF16)
+
+    mixed_back(7, a2)
+    total.start(OUT2)
+    sum_plan.now()
+    dq2 = active.at[pl.ds(0, D), pl.ds(0, rows)]
+    dk2 = active.at[pl.ds(D, D), pl.ds(0, sources)]
+    dv2 = active.at[pl.ds(D, D), pl.ds(rows, sources)]
+
+    def head_rows(ref):
+        def of(head):
+            return ref.at[pl.ds(pl.multiple_of(head * HEAD_DIM, HEAD_DIM), HEAD_DIM), :]
+
+        return of
+
+    sums = (r.key_sum, r.value_sum)
+    attention_backward(
+        q2,
+        k2,
+        v2,
+        grads,
+        [head_rows(ref) for ref in (dq2, dk2, dv2)],
+        sums,
+        r.shares,
+        r.score_grads,
+        cross_ranges,
+        sum_plan.loop(range(HEADS)),
+    )
+
+    def column_sum(index, value):
+        grad_columns[:, index : index + 1] += jnp.sum(value.astype(F32), axis=1, keepdims=True)
+
+    for tile in range(tiles):
+        gradient = res[span(tile), :] + dot(dq2[:, span(tile)], wide_column(4), 0, 1)
+        norm_back(0, tile, gradient, 2)
+        sum_plan.now()
+    shift[0:sources, :] = dot(dk2[...], wide_column(5), 0, 1) + dot(dv2[...], wide_column(6), 0, 1)
+    memory_copy = pltpu.make_async_copy(
+        shift.at[pl.ds(0, sources), :], r.grad_memory, local.at[10]
+    )
+    memory_copy.start()
+    wide[:, 5 * D : 6 * D] = dot(memory[...], dk2[...], 0, 1).astype(BF16)
+    wide[:, 6 * D : 7 * D] = dot(memory[...], dv2[...], 0, 1).astype(BF16)
+    total.start(KEYS2)
+    sum_plan.now()
+    wide[:, 4 * D : 5 * D] = dot(low[0][...], dq2[...], 0, 1).astype(BF16)
+    column_sum(3, dq2[...])
+    column_sum(4, dv2[...])
+    mixed_back(3, a)
+    total.start(MID)
+    sum_plan.now()
+
+    def pair_rows(block):
+        def of(head):
+            pair = head // 2
+            row = pair % 2 * PAIR + block * (PAIR // 3) + head % 2 * HEAD_DIM
+            start = pl.multiple_of(pair // 2 * rows, rows)
+            return active.at[pl.ds(pl.multiple_of(row, HEAD_DIM), HEAD_DIM), pl.ds(start, rows)]
+
+        return of
+
+    def pair_grad(pair):
+        return active[pair % 2 * PAIR : (pair % 2 + 1) * PAIR, pair // 2 * rows : (pair // 2 + 1) * rows]
+
+    def start_pair(pair):
+        where = (slice(None),) * net.count + (
+            slice(0, own_rows[1]),
+            slice(pair * PAIR, (pair + 1) * PAIR),
+        )
+        slope7[where] = (
+            dot(tokens[...], pair_grad(pair), 0, 1)
+            .astype(BF16)
+            .reshape(slope7.shape[: net.count] + (own_rows[1], PAIR))
+        )
+        if pair == HEADS // 2 - 1:
+            for other in range(HEADS // 2):
+                place = slice(other * bias_rows, (other + 1) * bias_rows)
+                grad = pair_grad(other).astype(F32)
+                for index, block in ((0, 0), (1, 2)):
+                    grad_columns[place, index : index + 1] = jnp.sum(
+                        grad[block * bias_rows : (block + 1) * bias_rows], axis=1, keepdims=True
+                    )
+            turned = jnp.transpose(r.grad_rows[...]) + grad_columns[...]
+            gvec7[...] = turned.reshape(gvec7.shape)
+        total.start(SELF + pair)
+
+    hooks = {}
+    for head in range(HEADS):
+        act = sum_plan.next()
+
+        def hook(head=head, act=act):
+            if head % 2 and head < HEADS - 1:
+                start_pair(head // 2)
+            if act:
+                act()
+
+        if act or (head % 2 and head < HEADS - 1):
+            hooks[head] = hook
+    attention_backward(
+        q,
+        k,
+        v,
+        grads,
+        [pair_rows(block) for block in range(3)],
+        sums,
+        r.shares,
+        r.score_grads,
+        self_ranges,
+        hooks,
+    )
+    start_pair(HEADS // 2 - 1)
+    sum_plan.now()
+    token_copies = []
+    for tile in range(tiles):
+        value = res[span(tile), :]
+        for side in range(2):
+            value = value + dot(
+                active[0 : 2 * PAIR, pl.ds(side * rows + tile * TILE, TILE)],
+                wide[:, 2 * side * PAIR : 2 * (side + 1) * PAIR],
+                0,
+                1,
+            )
+        res[span(tile), :] = value
+        copy = pltpu.make_async_copy(
+            res.at[span(tile), :], r.grad_tokens.at[span(tile), :], local.at[12 + tile]
+        )
+        copy.start()
+        token_copies.append(copy)
+        sum_plan.now()
+    sum_plan.now()
+    total.finish()
+    for copy in token_copies + [memory_copy]:
+        copy.wait()
+
+
+def finish_kernel(*refs):
+    given, results, held = refs[:12], refs[12:21], refs[21:33]
+    vec_out, semaphores = refs[33], refs[34]
+    loads = [
+        pltpu.make_async_copy(source, target, semaphores.at[index])
+        for index, (source, target) in enumerate(zip(given, held))
+    ]
+    for copy in loads:
+        copy.start()
+    stores = []
+
+    def store(index, source):
+        copy = pltpu.make_async_copy(source, results[index], semaphores.at[12 + index])
+        copy.start()
+        stores.append(copy)
+
+    for index in range(12):
+        loads[index].wait()
+        if index < 5:
+            store(index, held[index])
+        elif index == 5:
+            vec_out[...] = held[5][:, : vec_out.shape[1]]
+            store(5, vec_out)
+        elif index >= 9:
+            average = held[index - 3]
+            average[...] += (held[index][...].astype(F32) - average[...]) / AVG_STEPS
+            store(index - 3, average)
+    for copy in stores:
+        copy.wait()
+
+
+def fused_body(
+    wide_size,
+    narrow_size,
+    tokens,
+    memory,
+    w_wide,
+    w_tall,
+    vecs,
+    avg_wide,
+    avg_tall,
+    avg_vecs,
+    tgt_lengths,
+    src_lengths,
+    cotangent,
+):
+    count = (wide_size * narrow_size).bit_length() - 1
+    rows, sources = tokens.shape[0], memory.shape[0]
+    wide_rows, wide_columns = w_wide.shape
+    tall_rows = w_tall.shape[0]
+    vec_rows = vecs.shape[0]
+    bits = (2,) * count
+    hbm = pl.BlockSpec(memory_space=pl.ANY)
+    smem = pl.BlockSpec(memory_space=pltpu.SMEM)
+    inputs = dict(
+        tgt_lengths=tgt_lengths,
+        src_lengths=src_lengths,
+        tokens_in=tokens,
+        memory_in=memory,
+        cotangent=cotangent,
+        w_wide=w_wide,
+        w_tall=w_tall,
+        vecs=vecs,
+    )
+    outputs = dict(
+        slots=jax.ShapeDtypeStruct((rows, D), BF16),
+        grad_tokens=jax.ShapeDtypeStruct((rows, D), F32),
+        grad_memory=jax.ShapeDtypeStruct((sources, D), F32),
+        grad_wide=jax.ShapeDtypeStruct((wide_rows, wide_columns), F32),
+        grad_tall=jax.ShapeDtypeStruct((tall_rows, D), F32),
+        grad_vecs=jax.ShapeDtypeStruct((vec_rows, 128), F32),
+    )
+
+    def arrivals(shape, dtype=BF16):
+        line = (1 << (count - 3)) - 1
+        far = bits[3:]
+        return [
+            pltpu.VMEM(lead + shape, dtype) for lead in (bits[1:], far, far, far, (line,))
+        ]
+
+    scratch = dict(
+        wide=pltpu.VMEM(bits + (wide_rows, wide_columns), BF16),
+        tall=pltpu.VMEM(bits + (tall_rows, D), BF16),
+        vec=pltpu.VMEM(bits + vecs.shape, BF16),
+        grad_vec=pltpu.VMEM(bits + (vec_rows, 128), F32),
+        tokens=pltpu.VMEM((rows, D), BF16),
+        memory=pltpu.VMEM((sources, D), BF16),
+        seed=pltpu.VMEM((rows, D), BF16),
+        seed_next=pltpu.VMEM((rows, D), BF16),
+        q=pltpu.VMEM((HEADS, AUG, rows), BF16),
+        k=pltpu.VMEM((HEADS, AUG, rows), BF16),
+        v=pltpu.VMEM((HEADS, AUG, rows), BF16),
+        q2=pltpu.VMEM((HEADS, AUG, rows), BF16),
+        k2=pltpu.VMEM((HEADS, AUG, sources), BF16),
+        v2=pltpu.VMEM((HEADS, AUG, sources), BF16),
+        mixed_grad=pltpu.VMEM((HEADS, AUG, rows), BF16),
+        mixed=pltpu.VMEM((D, rows), BF16),
+        mixed2=pltpu.VMEM((D, rows), BF16),
+        active=pltpu.VMEM((rows, FF), BF16),
+        slope=pltpu.VMEM(bits + (rows >> count, FF), BF16),
+        res=pltpu.VMEM((rows, D), F32),
+        low_grad=pltpu.VMEM((rows, D), BF16),
+        shift=pltpu.VMEM((rows + 8, D), F32),
+        key_sum=pltpu.VMEM((HEAD_DIM, rows), F32),
+        value_sum=pltpu.VMEM((HEAD_DIM, rows), F32),
+        inverse=pltpu.VMEM((rows, 128), F32),
+        row_vectors=pltpu.VMEM((24, D), F32),
+        grad_rows=pltpu.VMEM((128, D), F32),
+        grad_columns=pltpu.VMEM((D, 128), F32),
+        out_wide=pltpu.VMEM((wide_rows, wide_columns), F32),
+        out_tall=pltpu.VMEM((tall_rows, D), F32),
+        out_vec=pltpu.VMEM((vec_rows, 128), F32),
+        normed=[pltpu.VMEM((rows, D), BF16) for _ in range(3)],
+        low=[pltpu.VMEM((rows, D), BF16) for _ in range(3)],
+        scores=[
+            pltpu.VMEM((max(high - low for low, high in bands(rows, rows, 512)), TILE), F32)
+            for _ in range(2)
+        ],
+        shares=[pltpu.VMEM((rows, TILE), BF16) for _ in range(2)],
+        score_grads=[pltpu.VMEM((rows, TILE), BF16) for _ in range(2)],
+        in_tall=[arrivals((tall_rows // TALL_CUT, D)) for _ in range(TALL_CUT)],
+        in_wide=[arrivals((wide_rows, blocks * D)) for blocks in (2, 2, 1, 2, 2)],
+        in_vec=arrivals((vec_rows, 128), F32),
+        local=pltpu.SemaphoreType.DMA((20,)),
+        own_done=pltpu.SemaphoreType.DMA((3 * HEADS // 2 + 1,)),
+        out_done=pltpu.SemaphoreType.DMA((OUT_SEMAPHORES,)),
+        gather_send=pltpu.SemaphoreType.DMA((6 + TALL_CUT, 3 + (1 << (count - 3)), 2)),
+        gather_receive=pltpu.SemaphoreType.DMA((6 + TALL_CUT, 3 + (1 << (count - 3)), 2)),
+        sum_send=pltpu.SemaphoreType.DMA((9 + TALL_CUT, 3 + (1 << (count - 3)), 2)),
+        sum_receive=pltpu.SemaphoreType.DMA((9 + TALL_CUT, 3 + (1 << (count - 3)), 2)),
+    )
+    scratch_leaves, scratch_tree = jax.tree.flatten(scratch)
+    input_leaves, output_leaves = list(inputs.values()), list(outputs.values())
+    names = list(inputs) + list(outputs)
+    spec = [smem if value.dtype == jnp.int32 else hbm for value in input_leaves]
+
+    def kernel(*refs):
+        held = dict(zip(names, refs))
+        held.update(jax.tree.unflatten(scratch_tree, refs[len(names) :]))
+        layer_kernel(types.SimpleNamespace(**held), wide_size, narrow_size)
+
+    slots, grad_tokens, grad_memory, grad_wide, grad_tall, grad_vecs = pl.pallas_call(
+        kernel,
+        out_shape=output_leaves,
+        in_specs=spec,
+        out_specs=[hbm] * len(outputs),
+        scratch_shapes=scratch_leaves,
+        compiler_params=pltpu.CompilerParams(
+            collective_id=0, has_side_effects=True, vmem_limit_bytes=67_000_000
+        ),
+    )(*input_leaves)
+    done = [slots, grad_tokens, grad_memory, grad_wide, grad_tall, grad_vecs]
+    done += [avg_wide, avg_tall, avg_vecs, w_wide, w_tall, vecs]
+    shapes = outputs | dict(grad_vecs=jax.ShapeDtypeStruct(vecs.shape, F32))
+    return pl.pallas_call(
+        finish_kernel,
+        out_shape=list(shapes.values())
+        + [jax.ShapeDtypeStruct(value.shape, F32) for value in (avg_wide, avg_tall, avg_vecs)],
+        in_specs=[hbm] * len(done),
+        out_specs=[hbm] * 9,
+        scratch_shapes=[pltpu.VMEM(value.shape, value.dtype) for value in done]
+        + [pltpu.VMEM(vecs.shape, F32), pltpu.SemaphoreType.DMA((21,))],
+    )(*done)
+
+
 def solution(mesh):
     in_specs = (
         P(("wide", "narrow"), None),
@@ -391,4 +1538,12 @@
         P(("wide", "narrow"), None),
         P(("wide", "narrow"), None),
     )
+    devices = mesh.shape["wide"] * mesh.shape["narrow"]
+    bits = devices.bit_length() - 1
+
+    def body(*args):
+        if args[2].shape[0] % 16 or args[3].shape[0] % 16 or devices != 1 << bits or bits < 3:
+            return plain_body(*args)
+        return fused_body(mesh.shape["wide"], mesh.shape["narrow"], *args)
+
     return jax.shard_map(body, mesh=mesh, in_specs=in_specs, out_specs=out_specs, check_vma=False)

time: 848 us -> 165 us (0.19)
  waiting for transfers between devices: 414 us -> 0 us
  matrix products: 209 us -> 0 us
  Pallas kernels: 0 us -> 161 us
  local copies, waits for them, and re-layouts: 81.1 us -> 0 us
  other arithmetic: 71.9 us -> 0 us
  blocking collectives: 43.8 us -> 0 us
  between operations: 15 us -> 0.86 us
    reduce_scatter x2 -> x0, waiting for transfers between devices: 279 us -> none  [the longest x1 161 us: body(): lax.psum_scatter(grad_wide_all, ('wide', 'narrow'), scatter_dimension=0,...]
    dot_general x64 -> x0, matrix products: 209 us -> none  [the longest x12 42 us: matmul_last(): lax.dot_general(left, right, (((1,), (1,)), ((), ())), preferred_element_...]
    pallas_call x0 -> x2, Pallas kernels: none -> 161 us  [the longest x1 157 us: fused_body(): pl.pallas_call(kernel, out_shape=output_leaves, in_specs=spec, out_specs=...]
    all_gather x2 -> x0, waiting for transfers between devices: 78.1 us -> none  [the longest x1 67.9 us: body(): lax.all_gather(w_wide, ('wide', 'narrow'), axis=0, tiled=True)]
    unnamed x6 -> x0, waiting for transfers between devices: 57.6 us -> none
    all_gather x1 -> x0, blocking collectives: 43.8 us -> none  [body(): lax.all_gather(vecs, ('wide', 'narrow'), axis=0, tiled=True)]
    reduce_sum x17 -> x0, other arithmetic: 27.3 us -> none  [the longest x4 11.9 us: attend_block(): totals = jnp.sum(exponent, axis=-1, keepdims=True)]
    convert_element_type x8 -> x0, other arithmetic: 26.6 us -> none  [the longest x4 23.9 us: backward_block(): score_grad = (shares * (share_grad - inner_sum)).astype(jnp.bfloat16)]
  transfers between devices with their start and end apart: 5 -> 0, of which waited for: 5 -> 0; matrix products, arithmetic and copies ran while one was open for 10% -> 0% of each run, Pallas kernels for 0% -> 0%
where the time goes in v1:
time: 165 us; the launch traced here: 162 us
  Pallas kernels  161 us (98%)
    pallas_call x1, Pallas kernels, fused_body(): pl.pallas_call(kernel, out_shape=output_leaves, in_specs=spec, out_specs=...  157 us
    pallas_call x1, Pallas kernels, fused_body(): pl.pallas_call(finish_kernel, out_shape=list(shapes.values()) + [jax.Shap...  4.32 us

profile of v1, /device:TPU:0, one launch (start us, length us, event | category | flops | bytes accessed | tf_op | source)
XLA Modules:
  0.0 161.7 jit_solution(2860422792301055031)
XLA Ops:
  0.6 156.5 %shard_map.178 = (bf16[1024,512]{1,0:T(8,128)(2,1)}, f32[1024,512]{1,0:T(8,128)}, f32[512,512]{1,0:T(8,128)}, f32[16,6144]{1,0:T(8,128)}, f32[96,512]{1,0:T(8,128)}, /*index=5*/f32[16,128]{1,0:T(8,128)}) custom-call(s32[1,6]{1,0:T(1,128)} %refs_0_.1, s32[1,6]{1,0:T(1,128)} %refs_1_.1, bf16[1024,512]{1,0:T(8,128)(2,1)} %refs_2_.1, bf16[512,512]{1,0:T(8,128)(2,1)} %refs_3_.1, ...), custom_call_target="tpu_custom_call" | custom-call | tf_op jit(solution)/shard_map/pallas_call | solution.py:1492
  157.2 4.3 %shard_map.179 = (bf16[1024,512]{1,0:T(8,128)(2,1)}, f32[1024,512]{1,0:T(8,128)}, f32[512,512]{1,0:T(8,128)}, f32[16,6144]{1,0:T(8,128)}, f32[96,512]{1,0:T(8,12...) custom-call(bf16[1024,512]{1,0:T(8,128)(2,1)} %get-tuple-element.15.refs_0_, ...), custom_call_target="tpu_custom_call" | custom-call | tf_op jit(solution)/shard_map/pallas_call | solution.py:1505

commit v2 on v1

--- a/solution.py
+++ b/solution.py
@@ -380,62 +380,52 @@
 TALL_CUT = 3
 OUT_SEMAPHORES = 24
 PAIR = 6 * HEAD_DIM
+PAIR_GROUPS = ((0,), (1,), (2, 3))
 GATHER_STEPS = {
-    4: ((0, 0), (1, 0), (0, 1), (2, 0), (1, 1), (0, 2), (3, 0), (0, 3),),
-    5: ((2, 1),),
-    8: ((4, 0),),
-    10: ((1, 2),),
-    13: ((3, 1),),
-    14: ((1, 3),),
-    18: ((5, 0),),
-    20: ((2, 2),),
-    23: ((4, 1),),
-    24: ((2, 3), (6, 0),),
-    29: ((3, 2),),
-    31: ((7, 0),),
-    33: ((3, 3),),
-    34: ((5, 1),),
-    37: ((8, 0),),
-    42: ((4, 2),),
-    44: ((6, 1),),
-    46: ((4, 3),),
-    54: ((7, 1),),
-    69: ((5, 2),),
-    75: ((8, 1),),
-    79: ((5, 3),),
-    81: ((6, 2),),
-    83: ((7, 2), (6, 3),),
-    84: ((8, 2), (7, 3), (8, 3),),
+    0: ((0, 0),),
+    1: ((0, 1), (1, 0), (0, 2), (1, 1), (2, 0), (0, 3),),
+    4: ((3, 0),),
+    5: ((1, 2), (2, 1), (1, 3),),
+    7: ((4, 0),),
+    9: ((3, 1), (5, 0), (2, 2), (2, 3),),
+    11: ((4, 1),),
+    12: ((6, 0), (3, 2),),
+    13: ((5, 1), (7, 0),),
+    14: ((3, 3),),
+    16: ((4, 2),),
+    19: ((6, 1),),
+    20: ((4, 3),),
+    21: ((8, 0),),
+    23: ((5, 2), (9, 0),),
+    25: ((7, 1),),
+    26: ((5, 3),),
+    28: ((6, 2),),
+    30: ((8, 1), (6, 3),),
+    33: ((9, 1),),
+    35: ((7, 2), (8, 2), (7, 3), (8, 3), (9, 2), (9, 3),),
 }
 SUM_STEPS = {
-    2: ((0, 0), (1, 0),),
-    3: ((2, 0),),
-    7: ((0, 1),),
-    8: ((3, 0),),
-    9: ((4, 0), (1, 1),),
-    10: ((5, 0), (2, 1),),
-    11: ((0, 2),),
-    12: ((3, 1),),
-    13: ((4, 1),),
-    14: ((0, 3),),
-    15: ((1, 2), (5, 1),),
-    16: ((2, 2),),
-    17: ((3, 2),),
-    19: ((4, 2),),
-    20: ((5, 2),),
-    21: ((1, 3),),
-    23: ((7, 0), (2, 3),),
-    24: ((6, 0), (3, 3),),
-    25: ((4, 3), (7, 1),),
-    26: ((5, 3), (8, 0),),
-    27: ((6, 1), (7, 2),),
-    28: ((9, 0), (8, 1),),
-    29: ((6, 2), (10, 0),),
-    30: ((7, 3), (9, 1),),
-    31: ((8, 2), (10, 1),),
-    33: ((6, 3), (11, 0),),
-    34: ((9, 2),),
-    36: ((10, 2), (8, 3), (11, 1), (9, 3), (10, 3), (11, 2), (11, 3),),
+    3: ((0, 0), (1, 0),),
+    4: ((2, 0),),
+    9: ((3, 0), (4, 0),),
+    10: ((0, 1), (5, 0),),
+    11: ((1, 1),),
+    13: ((2, 1),),
+    15: ((3, 1),),
+    21: ((4, 1),),
+    23: ((7, 0), (0, 2),),
+    24: ((6, 0), (5, 1),),
+    25: ((1, 2), (2, 2),),
+    26: ((8, 0), (3, 2),),
+    27: ((0, 3), (4, 2),),
+    28: ((7, 1), (9, 0),),
+    29: ((1, 3), (6, 1),),
+    30: ((10, 0), (5, 2),),
+    31: ((2, 3), (8, 1),),
+    32: ((7, 2), (3, 3),),
+    33: ((9, 1), (11, 0),),
+    35: ((6, 2),),
+    36: ((10, 1), (4, 3), (8, 2), (5, 3), (9, 2), (11, 1), (10, 2), (7, 3), (11, 2), (6, 3), (8, 3), (9, 3), (10, 3), (11, 3),),
 }
 
 
@@ -523,9 +513,8 @@
                 SEGS,
                 split_three(-(highest + jnp.log(total))),
             ).astype(BF16)
-            for at, hook in hooks.items():
-                if at[1] == tile:
-                    pl.when(head == at[0])(hook)
+        for at, hook in hooks.items():
+            pl.when(head == at)(hook)
         return carried
 
     lax.fori_loop(heads[0], heads[1], one_head, 0)
@@ -583,6 +572,8 @@
         self.own = tuple(self.bits[bit] for bit in reversed(range(self.count)))
         self.far = list(range(3, self.count))
         self.masks = [1, 2, 4] + [other << 3 for other in range(1, self.line)]
+        core = self.bits[0]
+        self.first, self.second, self.both = {1: 1 - core, 2: core}, {1: core, 2: 1 - core}, {1: 1, 2: 1}
 
     def device(self, mask):
         wide, narrow = self.place
@@ -598,21 +589,22 @@
     def meet(self):
         pl.semaphore_wait(pltpu.get_barrier_semaphore(), len(self.masks))
 
-    def by_core(self, split, act):
-        if split:
-            pl.when(self.bits[0] == 0)(lambda: act((1, 2)))
-            pl.when(self.bits[0] == 1)(lambda: act((2, 1)))
-        else:
-            act((1, 2))
-
-    def view(self, part, open_bits, flipped=0):
+    def neighbour(self, second):
+        core = self.bits[0]
+        take = core if not second else 1 - core
+        one, other = self.device(2), self.device(4)
+        return tuple(a + (b - a) * take for a, b in zip(one, other))
+
+    def view(self, part, open_bits, flips=None):
         index = tuple(
-            slice(None)
-            if bit in open_bits
-            else (1 - self.bits[bit] if flipped >> bit & 1 else self.bits[bit])
+            slice(None) if bit in open_bits else self.turned(bit, flips)
             for bit in reversed(range(self.count))
         )
         return part.ref.at[index + part.where]
+
+    def turned(self, bit, flips):
+        flip = (flips or {}).get(bit, 0)
+        return self.bits[bit] + flip - 2 * self.bits[bit] * flip
 
 
 class Part:
@@ -624,16 +616,27 @@
 class Transfer:
     def __init__(self, net, pieces, send, receive):
         self.net, self.pieces, self.send, self.receive = net, pieces, send, receive
-
-    def copy(self, piece, part, slot, source, target, mask):
+        line = tuple(range(4, 3 + net.line))
+        self.stages = (line, (0,), (1, 2), (3,)) if isinstance(self, Gather) else ((0,), (1,), (2, 3), line)
+
+    def copy(self, piece, part, slot, source, target, device):
         return pltpu.make_async_remote_copy(
             source,
             target,
             self.send.at[piece, slot, part],
             self.receive.at[piece, slot, part],
-            device_id=self.net.device(mask),
+            device_id=device,
             device_id_type=MESH_IDS,
         )
+
+    def each(self, piece, stage, act):
+        for number in range(len(self.pieces[piece])):
+            for slot in self.stages[stage]:
+                act(self.one(piece, number, slot))
+
+    def begin(self, piece, slot):
+        for number in range(len(self.pieces[piece])):
+            self.one(piece, number, slot).start()
 
     def finish(self):
         for piece in range(len(self.pieces)):
@@ -642,145 +645,96 @@
 
 
 class Gather(Transfer):
-    def each(self, piece, stage, act):
-        net = self.net
-
-        def with_order(near):
-            first, second = near
-            for number, part in enumerate(self.pieces[piece]):
-                if stage == 0:
-                    for other in range(1, net.line):
-                        view = net.view(part, [])
-                        act(self.copy(piece, number, other + 3, view, view, other << 3))
-                elif stage == 1:
-                    view = net.view(part, net.far)
-                    act(self.copy(piece, number, 0, view, view, 1 << first))
-                elif stage == 2:
-                    view = net.view(part, net.far)
-                    act(self.copy(piece, number, 1, view, view, 1 << second))
-                    view = net.view(part, net.far, 1 << first)
-                    act(self.copy(piece, number, 2, view, view, 1 << second))
-                else:
-                    view = net.view(part, net.far + [1, 2])
-                    act(self.copy(piece, number, 3, view, view, 1))
-
-        net.by_core(stage in (1, 2), with_order)
+    def one(self, piece, number, slot):
+        net, part = self.net, self.pieces[piece][number]
+        if slot == 3:
+            view, device = net.view(part, net.far + [1, 2]), net.device(1)
+        elif slot > 3:
+            view, device = net.view(part, []), net.device((slot - 3) << 3)
+        else:
+            view = net.view(part, net.far, net.first if slot == 2 else None)
+            device = net.neighbour(slot > 0)
+        return self.copy(piece, number, slot, view, view, device)
 
     def start(self, piece):
         if piece < len(self.pieces):
             self.each(piece, 0, lambda copy: copy.start())
 
     def step(self, piece, stage):
-        net = self.net
         self.each(piece, stage, lambda copy: copy.wait_recv())
         if stage == 0:
-            self.each(piece, 1, lambda copy: copy.start())
-            self.send_second(piece, 0)
+            self.begin(piece, 0)
+            self.begin(piece, 1)
+            if piece == 0:
+                self.start(1)
             self.start(piece + 2)
         elif stage == 1:
-            self.send_second(piece, 1)
+            self.begin(piece, 2)
         elif stage == 2:
-            self.each(piece, 3, lambda copy: copy.start())
-
-    def send_second(self, piece, which):
-        net = self.net
-
-        def with_order(near):
-            first, second = near
-            for number, part in enumerate(self.pieces[piece]):
-                view = net.view(part, net.far, which << first)
-                self.copy(piece, number, 1 + which, view, view, 1 << second).start()
-
-        net.by_core(True, with_order)
+            self.begin(piece, 3)
 
 
 class Sum(Transfer):
-    def each(self, piece, stage, act):
-        net = self.net
-
-        def with_order(near):
-            first, second = near
-            for number, part in enumerate(self.pieces[piece]):
-                arrive = part.buffers
-                if stage == 0:
-                    view = net.view(part, net.far + [1, 2], 1)
-                    act(self.copy(piece, number, 0, view, arrive[0], 1))
-                elif stage == 1:
-                    view = net.view(part, net.far, (1 << first) | (1 << second))
-                    act(self.copy(piece, number, 1, view, arrive[1], 1 << second))
-                elif stage == 2:
-                    view = net.view(part, net.far, 1 << second)
-                    act(self.copy(piece, number, 2, view, arrive[2], 1 << second))
-                    view = net.view(part, net.far, 1 << first)
-                    act(self.copy(piece, number, 3, view, arrive[3], 1 << first))
-                else:
-                    for other in range(1, net.line):
-                        view = net.view(part, [], other << 3)
-                        act(self.copy(piece, number, other + 3, view, arrive[4].at[other - 1], other << 3))
-
-        net.by_core(stage in (1, 2), with_order)
-
-    def send_one(self, piece, which):
-        net = self.net
-
-        def with_order(near):
-            bit = near[1 - which]
-            for number, part in enumerate(self.pieces[piece]):
-                view = net.view(part, net.far, 1 << bit)
-                self.copy(
-                    piece, number, 2 + which, view, part.buffers[2 + which], 1 << bit
-                ).start()
-
-        net.by_core(True, with_order)
+    def one(self, piece, number, slot):
+        net, part = self.net, self.pieces[piece][number]
+        if slot == 0:
+            view, device = net.view(part, net.far + [1, 2], {0: 1}), net.device(1)
+        elif slot > 3:
+            mask = (slot - 3) << 3
+            view, device = net.view(part, [], {bit: mask >> bit & 1 for bit in net.far}), net.device(mask)
+        else:
+            view = net.view(part, net.far, (None, net.both, net.second, net.first)[slot])
+            device = net.neighbour(slot < 3)
+        target = part.buffers[4].at[slot - 4] if slot > 3 else part.buffers[slot]
+        return self.copy(piece, number, slot, view, target, device)
 
     def start(self, piece):
-        self.each(piece, 0, lambda copy: copy.start())
+        self.begin(piece, 0)
 
     def add(self, piece, stage):
         net = self.net
-
-        def with_order(near):
-            rest = sorted(net.far + ([1, 2] if stage == 0 else []))
-            flipped = near[0] if stage == 1 else None
-
-            def one_shard(step, carried):
-                place = {bit: (step >> at) & 1 for at, bit in enumerate(rest)}
-                index = tuple(
-                    place[bit]
-                    if bit in place
-                    else (1 - net.bits[bit] if bit == flipped else net.bits[bit])
-                    for bit in reversed(range(net.count))
-                )
-                arrived = tuple(place[bit] for bit in reversed(rest)) + (slice(None), slice(None))
-                for part in self.pieces[piece]:
-                    where = index + part.where
-                    value = part.ref[where].astype(F32)
-                    for buffer in part.buffers[2:4] if stage == 2 else part.buffers[stage : stage + 1]:
-                        value = value + buffer[arrived].astype(F32)
-                    part.ref[where] = value.astype(part.ref.dtype)
-                return carried
-
-            lax.fori_loop(0, 1 << len(rest), one_shard, 0)
-
-        if stage < 3:
-            net.by_core(stage == 1, with_order)
+        if stage == 3:
+            for part in self.pieces[piece]:
+                value = part.ref[net.own + part.where].astype(F32)
+                for other in range(1, net.line):
+                    value = value + part.buffers[4][other - 1].astype(F32)
+                for low, high, staged, out, semaphore in part.outs:
+                    staged[...] = value[:, low:high]
+                    pltpu.make_async_copy(staged, out, semaphore).start()
             return
-        for part in self.pieces[piece]:
-            value = part.ref[net.own + part.where].astype(F32)
-            for other in range(1, net.line):
-                value = value + part.buffers[4][other - 1].astype(F32)
-            for low, high, staged, out, semaphore in part.outs:
-                staged[...] = value[:, low:high]
-                pltpu.make_async_copy(staged, out, semaphore).start()
+        rest = net.far + ([1, 2] if stage == 0 else [])
+        rest.sort()
+
+        def one_shard(step, carried):
+            place = {bit: (step >> at) & 1 for at, bit in enumerate(rest)}
+            index = tuple(
+                place[bit] if bit in place else net.turned(bit, net.first if stage == 1 else None)
+                for bit in reversed(range(net.count))
+            )
+            arrived = tuple(place[bit] for bit in reversed(rest)) + (slice(None), slice(None))
+            for part in self.pieces[piece]:
+                where = index + part.where
+                if stage == 2:
+                    value = (
+                        part.ref[where].astype(F32)
+                        + part.buffers[2][arrived].astype(F32)
+                        + part.buffers[3][arrived].astype(F32)
+                    )
+                else:
+                    value = part.ref[where] + part.buffers[stage][arrived]
+                part.ref[where] = value.astype(part.ref.dtype)
+            return carried
+
+        lax.fori_loop(0, 1 << len(rest), one_shard, 0, unroll=True)
 
     def step(self, piece, stage):
         self.each(piece, stage, lambda copy: copy.wait_recv())
         self.add(piece, stage)
         if stage == 0:
-            self.each(piece, 1, lambda copy: copy.start())
-            self.send_one(piece, 0)
+            self.begin(piece, 1)
+            self.begin(piece, 2)
         elif stage == 1:
-            self.send_one(piece, 1)
+            self.begin(piece, 3)
         elif stage == 2:
             self.each(piece, 3, lambda copy: copy.start())
 
@@ -862,7 +816,8 @@
     gather = Gather(
         net,
         [
-            wide_part(0, 2 * PAIR) + [Part(vec7)],
+            wide_part(0, PAIR) + [Part(vec7)],
+            wide_part(PAIR, 2 * PAIR),
             wide_part(2 * PAIR, 4 * PAIR),
             wide_part(3 * D, 5 * D),
             wide_part(5 * D, 7 * D),
@@ -897,14 +852,8 @@
             wide_out(block * third, (block + 1) * third, block * D + pair * third)
             for block in range(3)
         ]
-        buffers = [
-            buffer.at[
-                (slice(None),) * (len(buffer.shape) - 1) + (pl.ds(pair % 2 * PAIR, PAIR),)
-            ]
-            for buffer in r.in_wide[pair // 2]
-        ]
         columns = (pair * PAIR, (pair + 1) * PAIR)
-        return [Part(slope7, own_rows, columns, buffers, outs)]
+        return [Part(slope7, own_rows, columns, r.in_self[pair], outs)]
 
     vec_sum = Part(gvec7, None, None, r.in_vec, [out_of(0, 128, r.out_vec, r.grad_vecs)])
     ranges_of_sum = ((8, 10), (10, 12), (7, 8), (3, 5), (5, 7))
@@ -964,8 +913,6 @@
     every_head(q2, query_features(target_ends, rows))
     every_head(k, key_features(target_ends, rows))
     every_head(k2, key_features(source_ends, sources))
-    gather.start(1)
-    plan.now()
     every_head(v, value_features(rows))
     every_head(v2, value_features(sources))
     plan.now()
@@ -993,7 +940,6 @@
         masked = seed[span(tile), :].astype(F32) * valid(tile)
         seed[span(tile), :] = masked.astype(BF16)
         shift[pl.ds(tile * TILE + 8, TILE), :] = masked * follow(tile)
-    plan.now()
     for tile in range(tiles):
         seed_next[span(tile), :] = shift[pl.ds(tile * TILE + 7, TILE), :].astype(BF16)
     shift[rows : rows + 8, :] = jnp.zeros((8, D), F32)
@@ -1001,7 +947,6 @@
     r.grad_columns[...] = jnp.zeros_like(r.grad_columns)
     loads[-3].wait()
     loads[-2].wait()
-    plan.now()
 
     def row(index):
         return r.row_vectors[index : index + 1, :]
@@ -1021,36 +966,36 @@
     self_ranges = bands(rows, rows, 512)
     cross_ranges = bands(rows, sources, None)
     a, a2 = r.mixed, r.mixed2
-    halves = [(index * HEADS // 2, (index + 1) * HEADS // 2) for index in range(2)]
-
     bias_rows = PAIR // 3
     identity = lax.broadcasted_iota(jnp.int32, (D, D), 0) == lax.broadcasted_iota(
         jnp.int32, (D, D), 1
     )
     identity = jnp.where(identity, 1.0, 0.0).astype(BF16)
-    for index, heads in enumerate(halves):
+    for index, pairs in enumerate(PAIR_GROUPS):
         plan.now()
         if index == 0:
             r.row_vectors[0 : vec7.shape[-1], :] = dot(
                 vec7[...].reshape(D, vec7.shape[-1]), identity, 0, 0
             )
-        columns = slice(2 * index * PAIR, 2 * (index + 1) * PAIR)
         biases = []
-        for pair in (2 * index, 2 * index + 1):
+        for pair in pairs:
             place = slice(pair * bias_rows, (pair + 1) * bias_rows)
             biases += [column(0)[place], jnp.zeros((bias_rows, 1), F32), column(1)[place]]
         bias = jnp.concatenate(biases, axis=0)
         for tile in range(tiles):
-            both = (dot(wide[:, columns], tokens[span(tile), :], 0, 1) + bias).astype(BF16)
-            for pair in range(2):
-                group = slice(heads[0] + 2 * pair, heads[0] + 2 * pair + 2)
+            both = dot(
+                wide[:, pairs[0] * PAIR : (pairs[-1] + 1) * PAIR], tokens[span(tile), :], 0, 1
+            )
+            both = (both + bias).astype(BF16)
+            for place, pair in enumerate(pairs):
                 for block, ref in enumerate((q, k, v)):
-                    start = pair * PAIR + block * bias_rows
+                    start = place * PAIR + block * bias_rows
                     value = both[start : start + bias_rows]
                     if block == 0:
                         value = (value.astype(F32) * SCORE_SCALE).astype(BF16)
-                    ref[group, 0:HEAD_DIM, span(tile)] = heads_of(value)
+                    ref[2 * pair : 2 * pair + 2, 0:HEAD_DIM, span(tile)] = heads_of(value)
         plan.now()
+        heads = (2 * pairs[0], 2 * pairs[-1] + 2)
         attention_forward(
             q,
             k,
@@ -1059,7 +1004,7 @@
             r.scores,
             self_ranges,
             heads,
-            plan.loop([(head, tile) for head in range(*heads) for tile in range(tiles)]),
+            plan.loop(range(*heads)),
         )
 
     normed, low, inverse = r.normed, r.low, r.inverse
@@ -1097,7 +1042,7 @@
         r.scores,
         cross_ranges,
         (0, HEADS),
-        plan.loop([(head, tile) for head in range(HEADS) for tile in range(tiles)]),
+        plan.loop(range(HEADS)),
     )
     active = r.active
     plan.now()
@@ -1470,12 +1415,13 @@
         score_grads=[pltpu.VMEM((rows, TILE), BF16) for _ in range(2)],
         in_tall=[arrivals((tall_rows // TALL_CUT, D)) for _ in range(TALL_CUT)],
         in_wide=[arrivals((wide_rows, blocks * D)) for blocks in (2, 2, 1, 2, 2)],
+        in_self=[arrivals((wide_rows, PAIR)) for _ in range(HEADS // 2)],
         in_vec=arrivals((vec_rows, 128), F32),
         local=pltpu.SemaphoreType.DMA((20,)),
         own_done=pltpu.SemaphoreType.DMA((3 * HEADS // 2 + 1,)),
         out_done=pltpu.SemaphoreType.DMA((OUT_SEMAPHORES,)),
-        gather_send=pltpu.SemaphoreType.DMA((6 + TALL_CUT, 3 + (1 << (count - 3)), 2)),
-        gather_receive=pltpu.SemaphoreType.DMA((6 + TALL_CUT, 3 + (1 << (count - 3)), 2)),
+        gather_send=pltpu.SemaphoreType.DMA((7 + TALL_CUT, 3 + (1 << (count - 3)), 2)),
+        gather_receive=pltpu.SemaphoreType.DMA((7 + TALL_CUT, 3 + (1 << (count - 3)), 2)),
         sum_send=pltpu.SemaphoreType.DMA((9 + TALL_CUT, 3 + (1 << (count - 3)), 2)),
         sum_receive=pltpu.SemaphoreType.DMA((9 + TALL_CUT, 3 + (1 << (count - 3)), 2)),
     )

time: 165 us -> 154 us (0.933)
  Pallas kernels: 161 us -> 150 us
    pallas_call x1, Pallas kernels: 157 us -> 146 us  [fused_body(): pl.pallas_call(kernel, out_shape=output_leaves, in_specs=spec, out_specs=...]
where the time goes in v2:
time: 154 us; the launch traced here: 151 us
  Pallas kernels  150 us (97%)
    pallas_call x1, Pallas kernels, fused_body(): pl.pallas_call(kernel, out_shape=output_leaves, in_specs=spec, out_specs=...  146 us
    pallas_call x1, Pallas kernels, fused_body(): pl.pallas_call(finish_kernel, out_shape=list(shapes.values()) + [jax.Shap...  4.32 us

profile of v2, /device:TPU:0, one launch (start us, length us, event | category | flops | bytes accessed | tf_op | source)
XLA Modules:
  0.0 151.1 jit_solution(12705204643817598562)
XLA Ops:
  0.6 146.0 %shard_map.178 = (bf16[1024,512]{1,0:T(8,128)(2,1)}, f32[1024,512]{1,0:T(8,128)}, f32[512,512]{1,0:T(8,128)}, f32[16,6144]{1,0:T(8,128)}, f32[96,512]{1,0:T(8,128)}, /*index=5*/f32[16,128]{1,0:T(8,128)}) custom-call(s32[1,6]{1,0:T(1,128)} %refs_0_.1, s32[1,6]{1,0:T(1,128)} %refs_1_.1, bf16[1024,512]{1,0:T(8,128)(2,1)} %refs_2_.1, bf16[512,512]{1,0:T(8,128)(2,1)} %refs_3_.1, ...), custom_call_target="tpu_custom_call" | custom-call | tf_op jit(solution)/shard_map/pallas_call | solution.py:1438
  146.6 4.3 %shard_map.179 = (bf16[1024,512]{1,0:T(8,128)(2,1)}, f32[1024,512]{1,0:T(8,128)}, f32[512,512]{1,0:T(8,128)}, f32[16,6144]{1,0:T(8,128)}, f32[96,512]{1,0:T(8,12...) custom-call(bf16[1024,512]{1,0:T(8,128)(2,1)} %get-tuple-element.15.refs_0_, ...), custom_call_target="tpu_custom_call" | custom-call | tf_op jit(solution)/shard_map/pallas_call | solution.py:1451

commit v3 on v2

--- a/solution.py
+++ b/solution.py
@@ -383,49 +383,45 @@
 PAIR_GROUPS = ((0,), (1,), (2, 3))
 GATHER_STEPS = {
     0: ((0, 0),),
-    1: ((0, 1), (1, 0), (0, 2), (1, 1), (2, 0), (0, 3),),
+    1: ((1, 0), (0, 2), (1, 1), (2, 0), (0, 3),),
+    2: ((9, 0),),
     4: ((3, 0),),
     5: ((1, 2), (2, 1), (1, 3),),
     7: ((4, 0),),
     9: ((3, 1), (5, 0), (2, 2), (2, 3),),
     11: ((4, 1),),
-    12: ((6, 0), (3, 2),),
+    12: ((6, 0), (9, 1), (3, 2),),
     13: ((5, 1), (7, 0),),
     14: ((3, 3),),
     16: ((4, 2),),
     19: ((6, 1),),
     20: ((4, 3),),
     21: ((8, 0),),
-    23: ((5, 2), (9, 0),),
+    23: ((5, 2),),
     25: ((7, 1),),
     26: ((5, 3),),
     28: ((6, 2),),
     30: ((8, 1), (6, 3),),
-    33: ((9, 1),),
-    35: ((7, 2), (8, 2), (7, 3), (8, 3), (9, 2), (9, 3),),
+    32: ((9, 2),),
+    33: ((7, 2),),
+    35: ((9, 3), (8, 2), (7, 3), (8, 3),),
 }
 SUM_STEPS = {
-    3: ((0, 0), (1, 0),),
-    4: ((2, 0),),
-    9: ((3, 0), (4, 0),),
-    10: ((0, 1), (5, 0),),
-    11: ((1, 1),),
-    13: ((2, 1),),
-    15: ((3, 1),),
-    21: ((4, 1),),
-    23: ((7, 0), (0, 2),),
-    24: ((6, 0), (5, 1),),
-    25: ((1, 2), (2, 2),),
-    26: ((8, 0), (3, 2),),
-    27: ((0, 3), (4, 2),),
-    28: ((7, 1), (9, 0),),
-    29: ((1, 3), (6, 1),),
-    30: ((10, 0), (5, 2),),
-    31: ((2, 3), (8, 1),),
-    32: ((7, 2), (3, 3),),
-    33: ((9, 1), (11, 0),),
-    35: ((6, 2),),
-    36: ((10, 1), (4, 3), (8, 2), (5, 3), (9, 2), (11, 1), (10, 2), (7, 3), (11, 2), (6, 3), (8, 3), (9, 3), (10, 3), (11, 3),),
+    5: ((0, 0),),
+    10: ((1, 0),),
+    12: ((0, 1),),
+    16: ((1, 1),),
+    24: ((0, 2), (2, 0),),
+    25: ((1, 2), (3, 0),),
+    27: ((4, 0), (2, 1),),
+    29: ((3, 1), (0, 3),),
+    30: ((5, 0), (4, 1),),
+    34: ((2, 2),),
+    35: ((3, 2), (6, 0),),
+    36: ((1, 3), (7, 0),),
+    40: ((5, 1),),
+    42: ((4, 2),),
+    44: ((6, 1), (7, 1), (5, 2), (6, 2), (7, 2), (2, 3), (3, 3), (4, 3), (5, 3), (6, 3), (7, 3),),
 }
 
 
@@ -571,7 +567,7 @@
         self.bits = [(number >> bit) & 1 for bit in range(self.count)]
         self.own = tuple(self.bits[bit] for bit in reversed(range(self.count)))
         self.far = list(range(3, self.count))
-        self.masks = [1, 2, 4] + [other << 3 for other in range(1, self.line)]
+        self.masks = [1, 2, 4, 6] + [other << 3 for other in range(1, self.line)]
         core = self.bits[0]
         self.first, self.second, self.both = {1: 1 - core, 2: core}, {1: core, 2: 1 - core}, {1: 1, 2: 1}
 
@@ -616,8 +612,7 @@
 class Transfer:
     def __init__(self, net, pieces, send, receive):
         self.net, self.pieces, self.send, self.receive = net, pieces, send, receive
-        line = tuple(range(4, 3 + net.line))
-        self.stages = (line, (0,), (1, 2), (3,)) if isinstance(self, Gather) else ((0,), (1,), (2, 3), line)
+        self.line = tuple(range(4, 3 + net.line))
 
     def copy(self, piece, part, slot, source, target, device):
         return pltpu.make_async_remote_copy(
@@ -631,7 +626,7 @@
 
     def each(self, piece, stage, act):
         for number in range(len(self.pieces[piece])):
-            for slot in self.stages[stage]:
+            for slot in self.slots(piece, stage):
                 act(self.one(piece, number, slot))
 
     def begin(self, piece, slot):
@@ -645,36 +640,61 @@
 
 
 class Gather(Transfer):
+    def __init__(self, net, pieces, send, receive):
+        super().__init__(net, pieces, send, receive)
+        self.last = len(pieces) - 1
+
+    def slots(self, piece, stage):
+        if piece == 0:
+            return (self.line, (), (0, 1, 2), (3,))[stage]
+        if piece == self.last:
+            return ((0, 1), (2,), self.line, (3,))[stage]
+        return (self.line, (0,), (1, 2), (3,))[stage]
+
     def one(self, piece, number, slot):
         net, part = self.net, self.pieces[piece][number]
+        lines = [] if piece == self.last else net.far
         if slot == 3:
             view, device = net.view(part, net.far + [1, 2]), net.device(1)
         elif slot > 3:
-            view, device = net.view(part, []), net.device((slot - 3) << 3)
+            near = [1, 2] if piece == self.last else []
+            view, device = net.view(part, near), net.device((slot - 3) << 3)
+        elif slot == 2 and piece == 0:
+            view, device = net.view(part, lines), net.device(6)
         else:
-            view = net.view(part, net.far, net.first if slot == 2 else None)
+            view = net.view(part, lines, net.first if slot == 2 else None)
             device = net.neighbour(slot > 0)
         return self.copy(piece, number, slot, view, view, device)
 
     def start(self, piece):
-        if piece < len(self.pieces):
+        if piece == self.last:
+            self.begin(piece, 0)
+            self.begin(piece, 1)
+        else:
             self.each(piece, 0, lambda copy: copy.start())
 
     def step(self, piece, stage):
         self.each(piece, stage, lambda copy: copy.wait_recv())
-        if stage == 0:
+        if piece == self.last and stage < 2:
+            self.each(piece, stage + 1, lambda copy: copy.start())
+        elif stage == 0:
             self.begin(piece, 0)
             self.begin(piece, 1)
             if piece == 0:
+                self.begin(0, 2)
                 self.start(1)
-            self.start(piece + 2)
-        elif stage == 1:
+            if piece + 2 < self.last:
+                self.start(piece + 2)
+        elif stage == 1 and piece:
             self.begin(piece, 2)
         elif stage == 2:
             self.begin(piece, 3)
 
 
 class Sum(Transfer):
+    def slots(self, piece, stage):
+        return ((0,), (1,), (2, 3), self.line)[stage]
+
     def one(self, piece, number, slot):
         net, part = self.net, self.pieces[piece][number]
         if slot == 0:
@@ -838,11 +858,6 @@
         columns = pl.ds(start, high - low)
         return out_of(low, high, r.out_wide.at[:, columns], r.grad_wide.at[:, columns])
 
-    def tall_sum(cut, buffers):
-        place = pl.ds(cut[0], cut[1] - cut[0])
-        out = out_of(0, D, r.out_tall.at[place, :], r.grad_tall.at[place, :])
-        return [Part(tall7, cut, None, buffers, [out])]
-
     def wide_sum(low, high, buffers):
         return [Part(wide7, None, (low, high), buffers, [wide_out(0, high - low, low)])]
 
@@ -855,26 +870,28 @@
         columns = (pair * PAIR, (pair + 1) * PAIR)
         return [Part(slope7, own_rows, columns, r.in_self[pair], outs)]
 
-    vec_sum = Part(gvec7, None, None, r.in_vec, [out_of(0, 128, r.out_vec, r.grad_vecs)])
-    ranges_of_sum = ((8, 10), (10, 12), (7, 8), (3, 5), (5, 7))
+    vec_out = out_of(0, 128, r.out_vec, r.grad_vecs)
     total = Sum(
         net,
-        [tall_sum(cut, buffers) for cut, buffers in zip(tall_cuts, r.in_tall)]
-        + [
-            wide_sum(low * D, high * D, buffers)
-            for (low, high), buffers in zip(ranges_of_sum, r.in_wide)
+        [
+            [Part(tall7, None, None, r.in_tall, [out_of(0, D, r.out_tall, r.grad_tall)])],
+            wide_sum(8 * D, 12 * D, r.in_up),
+            wide_sum(3 * D, 8 * D, r.in_mid),
         ]
-        + [self_sum(pair) + ([vec_sum] if pair == HEADS // 2 - 1 else []) for pair in range(HEADS // 2)],
+        + [self_sum(pair) for pair in range(HEADS // 2)]
+        + [[Part(gvec7, None, None, r.in_vec, [vec_out])]],
         r.sum_send,
         r.sum_receive,
     )
-    TALL, UP, OUT2, MID, KEYS2, SELF = 0, TALL_CUT, TALL_CUT + 2, TALL_CUT + 3, TALL_CUT + 4, TALL_CUT + 5
+    TALL, UP, MID, SELF = range(4)
+    VECTORS = SELF + HEADS // 2
     sum_plan = Plan(total, SUM_STEPS)
 
     for copy in loads[:-3]:
         copy.wait()
     net.meet()
     gather.start(0)
+    gather.start(gather.last)
 
     def endings(lengths):
         found, running = [], 0
@@ -942,7 +959,6 @@
         shift[pl.ds(tile * TILE + 8, TILE), :] = masked * follow(tile)
     for tile in range(tiles):
         seed_next[span(tile), :] = shift[pl.ds(tile * TILE + 7, TILE), :].astype(BF16)
-    shift[rows : rows + 8, :] = jnp.zeros((8, D), F32)
     r.grad_rows[...] = jnp.zeros_like(r.grad_rows)
     r.grad_columns[...] = jnp.zeros_like(r.grad_columns)
     loads[-3].wait()
@@ -1066,24 +1082,8 @@
         before = (
             res[span(tile), :] + dot(active[span(tile), :], tall[0:FF, :], 1, 0) + row(BIAS_OUT)
         )
-        out = norm_tile(2, tile, before).astype(BF16)
-        shift[span(tile), :] = dot(out, slot_right[...], 1, 0)
+        norm_tile(2, tile, before)
     low_grad = r.low_grad
-    slot_copies = []
-    for tile in range(tiles):
-        low_grad[span(tile), :] = (
-            (
-                dot(low[2][span(tile), :], slot_left[...], 1, 0)
-                + follow(tile) * shift[pl.ds(tile * TILE + 1, TILE), :]
-                + row(BIAS_OUT + 1)
-            )
-            * valid(tile)
-        ).astype(BF16)
-        copy = pltpu.make_async_copy(
-            low_grad.at[span(tile), :], r.slots.at[span(tile), :], local.at[6 + tile]
-        )
-        copy.start()
-        slot_copies.append(copy)
     gather.finish()
 
     grad_rows, grad_columns = r.grad_rows, r.grad_columns
@@ -1111,10 +1111,13 @@
         gradient = dot(part, slot_left[...], 1, 1) + dot(
             seed_next[span(tile), :], slot_right[...], 1, 1
         )
-        slot_copies[tile].wait()
         norm_back(2, tile, gradient, BIAS_OUT)
-    slot_left[...] = dot(low[2][...], seed[...], 0, 0).astype(BF16)
-    slot_right[...] = dot(low[2][...], seed_next[...], 0, 0).astype(BF16)
+    grad_left = dot(low[2][...], seed[...], 0, 0).astype(BF16)
+    seed[0:D, :] = slot_left[...]
+    slot_left[...] = grad_left
+    grad_right = dot(low[2][...], seed_next[...], 0, 0).astype(BF16)
+    seed[D : 2 * D, :] = slot_right[...]
+    slot_right[...] = grad_right
     for block in range(FF // D):
         columns = slice(block * D, (block + 1) * D)
         for tile in range(tiles):
@@ -1124,8 +1127,7 @@
             add_row(6 + block, grad)
             slope[span(tile), columns] = grad.astype(BF16)
         tall[columns, :] = dot(active[:, columns], low_grad[...], 0, 0).astype(BF16)
-    for cut in range(TALL_CUT):
-        total.start(TALL + cut)
+    total.start(TALL)
     for tile in range(tiles):
         gradient = res[span(tile), :] + dot(
             slope[span(tile), :], wide[:, 8 * D : 8 * D + FF], 1, 1
@@ -1137,8 +1139,8 @@
         wide[:, 8 * D + block * D : 8 * D + (block + 1) * D] = dot(
             low[1][...], slope[:, columns], 0, 0
         ).astype(BF16)
-        if block % 2 == 1:
-            total.start(UP + block // 2)
+        if block == FF // D - 1:
+            total.start(UP)
         sum_plan.now()
     grads = r.mixed_grad
 
@@ -1161,7 +1163,6 @@
         ).astype(BF16)
 
     mixed_back(7, a2)
-    total.start(OUT2)
     sum_plan.now()
     dq2 = active.at[pl.ds(0, D), pl.ds(0, rows)]
     dk2 = active.at[pl.ds(D, D), pl.ds(0, sources)]
@@ -1201,7 +1202,6 @@
     memory_copy.start()
     wide[:, 5 * D : 6 * D] = dot(memory[...], dk2[...], 0, 1).astype(BF16)
     wide[:, 6 * D : 7 * D] = dot(memory[...], dv2[...], 0, 1).astype(BF16)
-    total.start(KEYS2)
     sum_plan.now()
     wide[:, 4 * D : 5 * D] = dot(low[0][...], dq2[...], 0, 1).astype(BF16)
     column_sum(3, dq2[...])
@@ -1232,17 +1232,19 @@
             .astype(BF16)
             .reshape(slope7.shape[: net.count] + (own_rows[1], PAIR))
         )
-        if pair == HEADS // 2 - 1:
-            for other in range(HEADS // 2):
-                place = slice(other * bias_rows, (other + 1) * bias_rows)
-                grad = pair_grad(other).astype(F32)
-                for index, block in ((0, 0), (1, 2)):
-                    grad_columns[place, index : index + 1] = jnp.sum(
-                        grad[block * bias_rows : (block + 1) * bias_rows], axis=1, keepdims=True
-                    )
-            turned = jnp.transpose(r.grad_rows[...]) + grad_columns[...]
-            gvec7[...] = turned.reshape(gvec7.shape)
         total.start(SELF + pair)
+
+    def start_vectors():
+        for pair in range(HEADS // 2):
+            place = slice(pair * bias_rows, (pair + 1) * bias_rows)
+            grad = pair_grad(pair).astype(F32)
+            for index, block in ((0, 0), (1, 2)):
+                grad_columns[place, index : index + 1] = jnp.sum(
+                    grad[block * bias_rows : (block + 1) * bias_rows], axis=1, keepdims=True
+                )
+        turned = jnp.transpose(r.grad_rows[...]) + grad_columns[...]
+        gvec7[...] = turned.reshape(gvec7.shape)
+        total.start(VECTORS)
 
     hooks = {}
     for head in range(HEADS):
@@ -1269,8 +1271,30 @@
         hooks,
     )
     start_pair(HEADS // 2 - 1)
+    start_vectors()
     sum_plan.now()
+
+    memory_copy.wait()
+    shift[rows : rows + 8, :] = jnp.zeros((8, D), F32)
+    for tile in range(tiles):
+        shift[span(tile), :] = dot(low[2][span(tile), :], seed[D : 2 * D, :], 1, 0)
+        sum_plan.now()
     token_copies = []
+    for tile in range(tiles):
+        low_grad[span(tile), :] = (
+            (
+                dot(low[2][span(tile), :], seed[0:D, :], 1, 0)
+                + follow(tile) * shift[pl.ds(tile * TILE + 1, TILE), :]
+                + row(BIAS_OUT + 1)
+            )
+            * valid(tile)
+        ).astype(BF16)
+        copy = pltpu.make_async_copy(
+            low_grad.at[span(tile), :], r.slots.at[span(tile), :], local.at[6 + tile]
+        )
+        copy.start()
+        token_copies.append(copy)
+        sum_plan.now()
     for tile in range(tiles):
         value = res[span(tile), :]
         for side in range(2):
@@ -1289,7 +1313,7 @@
         sum_plan.now()
     sum_plan.now()
     total.finish()
-    for copy in token_copies + [memory_copy]:
+    for copy in token_copies:
         copy.wait()
 
 
@@ -1413,8 +1437,9 @@
         ],
         shares=[pltpu.VMEM((rows, TILE), BF16) for _ in range(2)],
         score_grads=[pltpu.VMEM((rows, TILE), BF16) for _ in range(2)],
-        in_tall=[arrivals((tall_rows // TALL_CUT, D)) for _ in range(TALL_CUT)],
-        in_wide=[arrivals((wide_rows, blocks * D)) for blocks in (2, 2, 1, 2, 2)],
+        in_tall=arrivals((tall_rows, D)),
+        in_up=arrivals((wide_rows, FF)),
+        in_mid=arrivals((wide_rows, 5 * D)),
         in_self=[arrivals((wide_rows, PAIR)) for _ in range(HEADS // 2)],
         in_vec=arrivals((vec_rows, 128), F32),
         local=pltpu.SemaphoreType.DMA((20,)),
@@ -1422,8 +1447,8 @@
         out_done=pltpu.SemaphoreType.DMA((OUT_SEMAPHORES,)),
         gather_send=pltpu.SemaphoreType.DMA((7 + TALL_CUT, 3 + (1 << (count - 3)), 2)),
         gather_receive=pltpu.SemaphoreType.DMA((7 + TALL_CUT, 3 + (1 << (count - 3)), 2)),
-        sum_send=pltpu.SemaphoreType.DMA((9 + TALL_CUT, 3 + (1 << (count - 3)), 2)),
-        sum_receive=pltpu.SemaphoreType.DMA((9 + TALL_CUT, 3 + (1 << (count - 3)), 2)),
+        sum_send=pltpu.SemaphoreType.DMA((4 + HEADS // 2, 3 + (1 << (count - 3)), 1)),
+        sum_receive=pltpu.SemaphoreType.DMA((4 + HEADS // 2, 3 + (1 << (count - 3)), 1)),
     )
     scratch_leaves, scratch_tree = jax.tree.flatten(scratch)
     input_leaves, output_leaves = list(inputs.values()), list(outputs.values())

time: 154 us -> 146 us (0.948)
  Pallas kernels: 150 us -> 142 us
    pallas_call x1, Pallas kernels: 146 us -> 138 us  [fused_body(): pl.pallas_call(kernel, out_shape=output_leaves, in_specs=spec, out_specs=...]
where the time goes in v3:
time: 146 us; the launch traced here: 143 us
  Pallas kernels  142 us (97%)
    pallas_call x1, Pallas kernels, fused_body(): pl.pallas_call(kernel, out_shape=output_leaves, in_specs=spec, out_specs=...  138 us
    pallas_call x1, Pallas kernels, fused_body(): pl.pallas_call(finish_kernel, out_shape=list(shapes.values()) + [jax.Shap...  4.32 us

profile of v3, /device:TPU:0, one launch (start us, length us, event | category | flops | bytes accessed | tf_op | source)
XLA Modules:
  0.0 143.3 jit_solution(7328938502586543239)
XLA Ops:
  0.6 138.1 %shard_map.178 = (bf16[1024,512]{1,0:T(8,128)(2,1)}, f32[1024,512]{1,0:T(8,128)}, f32[512,512]{1,0:T(8,128)}, f32[16,6144]{1,0:T(8,128)}, f32[96,512]{1,0:T(8,128)}, /*index=5*/f32[16,128]{1,0:T(8,128)}) custom-call(s32[1,6]{1,0:T(1,128)} %refs_0_.1, s32[1,6]{1,0:T(1,128)} %refs_1_.1, bf16[1024,512]{1,0:T(8,128)(2,1)} %refs_2_.1, bf16[512,512]{1,0:T(8,128)(2,1)} %refs_3_.1, ...), custom_call_target="tpu_custom_call" | custom-call | tf_op jit(solution)/shard_map/pallas_call | solution.py:1463
  138.8 4.3 %shard_map.179 = (bf16[1024,512]{1,0:T(8,128)(2,1)}, f32[1024,512]{1,0:T(8,128)}, f32[512,512]{1,0:T(8,128)}, f32[16,6144]{1,0:T(8,128)}, f32[96,512]{1,0:T(8,12...) custom-call(bf16[1024,512]{1,0:T(8,128)(2,1)} %get-tuple-element.15.refs_0_, ...), custom_call_target="tpu_custom_call" | custom-call | tf_op jit(solution)/shard_map/pallas_call | solution.py:1476

commit v4 on v3

--- a/solution.py
+++ b/solution.py
@@ -410,17 +410,16 @@
     5: ((0, 0),),
     10: ((1, 0),),
     12: ((0, 1),),
-    16: ((1, 1),),
-    24: ((0, 2), (2, 0),),
-    25: ((1, 2), (3, 0),),
+    20: ((1, 1),),
+    24: ((2, 0), (0, 2),),
+    25: ((3, 0), (1, 2),),
     27: ((4, 0), (2, 1),),
-    29: ((3, 1), (0, 3),),
-    30: ((5, 0), (4, 1),),
-    34: ((2, 2),),
-    35: ((3, 2), (6, 0),),
-    36: ((1, 3), (7, 0),),
-    40: ((5, 1),),
-    42: ((4, 2),),
+    29: ((3, 1), (5, 0),),
+    30: ((4, 1), (0, 3),),
+    37: ((2, 2), (6, 0),),
+    38: ((7, 0), (3, 2),),
+    39: ((5, 1),),
+    40: ((1, 3), (4, 2),),
     44: ((6, 1), (7, 1), (5, 2), (6, 2), (7, 2), (2, 3), (3, 3), (4, 3), (5, 3), (6, 3), (7, 3),),
 }
 
@@ -431,9 +430,9 @@
     )
 
 
-def bands(query_rows, key_rows, longest):
+def bands(query_rows, key_rows, longest, tile=TILE):
     found = []
-    for start in range(0, query_rows, TILE):
+    for start in range(0, query_rows, tile):
         if longest is None:
             found.append((0, key_rows))
             continue
@@ -481,11 +480,12 @@
 
 def attention_forward(queries, keys, values, mixed, scores, ranges, heads, hooks):
     tiles = len(ranges)
+    width = queries.shape[2] // tiles
 
     def put(head, tile):
         low, high = ranges[tile]
         scores[tile % 2][0 : high - low, :] = dot(
-            keys[head, :, low:high], queries[head, :, tile * TILE : (tile + 1) * TILE], 0, 0
+            keys[head, :, low:high], queries[head, :, tile * width : (tile + 1) * width], 0, 0
         )
 
     put(heads[0], 0)
@@ -496,7 +496,7 @@
                 put(head, tile + 1)
             else:
                 put(jnp.minimum(head + 1, heads[1] - 1), 0)
-            span = slice(tile * TILE, (tile + 1) * TILE)
+            span = slice(tile * width, (tile + 1) * width)
             current = scores[tile % 2][0 : high - low, :]
             highest = column_max(current)
             shares = jnp.exp(current - highest).astype(BF16)
@@ -524,10 +524,10 @@
     def put(head, tile):
         low, high = ranges[tile]
         span = slice(tile * TILE, (tile + 1) * TILE)
-        share = jnp.exp(dot(keys[head, :, low:high], queries[head, :, span], 0, 0))
-        share_grad = dot(values[head, :, low:high], grads[head, :, span], 0, 0)
-        shares[tile % 2][0 : high - low, :] = share.astype(BF16)
-        score_grads[tile % 2][0 : high - low, :] = (share * share_grad).astype(BF16)
+        share = jnp.exp(dot(queries[head, :, span], keys[head, :, low:high], 0, 0))
+        share_grad = dot(grads[head, :, span], values[head, :, low:high], 0, 0)
+        shares[tile % 2][:, 0 : high - low] = share.astype(BF16)
+        score_grads[tile % 2][:, 0 : high - low] = (share * share_grad).astype(BF16)
 
     put(0, 0)
 
@@ -541,13 +541,13 @@
             else:
                 put(jnp.minimum(head + 1, HEADS - 1), 0)
             span = slice(tile * TILE, (tile + 1) * TILE)
-            share = shares[tile % 2][0 : high - low, :]
-            score_grad = score_grads[tile % 2][0 : high - low, :]
+            share = shares[tile % 2][:, 0 : high - low]
+            score_grad = score_grads[tile % 2][:, 0 : high - low]
             query_out[:, span] = (
-                dot(keys[head, 0:HEAD_DIM, low:high], score_grad, 1, 0) * SCORE_SCALE
+                dot(keys[head, 0:HEAD_DIM, low:high], score_grad, 1, 1) * SCORE_SCALE
             ).astype(BF16)
-            key_sum[:, low:high] += dot(queries[head, 0:HEAD_DIM, span], score_grad, 1, 1)
-            value_sum[:, low:high] += dot(grads[head, 0:HEAD_DIM, span], share, 1, 1)
+            key_sum[:, low:high] += dot(queries[head, 0:HEAD_DIM, span], score_grad, 1, 0)
+            value_sum[:, low:high] += dot(grads[head, 0:HEAD_DIM, span], share, 1, 0)
         key_out[...] = key_sum[:, 0:key_rows].astype(BF16)
         value_out[...] = value_sum[:, 0:key_rows].astype(BF16)
         for at, hook in hooks.items():
@@ -633,8 +633,8 @@
         for number in range(len(self.pieces[piece])):
             self.one(piece, number, slot).start()
 
-    def finish(self):
-        for piece in range(len(self.pieces)):
+    def finish(self, pieces=None):
+        for piece in range(len(self.pieces)) if pieces is None else pieces:
             for stage in range(4):
                 self.each(piece, stage, lambda copy: copy.wait_send())
 
@@ -981,6 +981,8 @@
 
     self_ranges = bands(rows, rows, 512)
     cross_ranges = bands(rows, sources, None)
+    cross_wide = bands(rows, sources, None, 2 * TILE)
+    cross_scores = [shift.at[pl.ds(start, sources), :] for start in (0, sources)]
     a, a2 = r.mixed, r.mixed2
     bias_rows = PAIR // 3
     identity = lax.broadcasted_iota(jnp.int32, (D, D), 0) == lax.broadcasted_iota(
@@ -1055,8 +1057,8 @@
         k2,
         v2,
         a2,
-        r.scores,
-        cross_ranges,
+        cross_scores,
+        cross_wide,
         (0, HEADS),
         plan.loop(range(HEADS)),
     )
@@ -1075,6 +1077,8 @@
             active[span(tile), columns] = value.astype(BF16)
             slope[span(tile), columns] = derivative.astype(BF16)
         plan.now()
+    early = range(gather.last - 2)
+    gather.finish(early)
     plan.now()
     slot_left = tall.at[pl.ds(FF, D), :]
     slot_right = tall.at[pl.ds(FF + D, D), :]
@@ -1084,7 +1088,7 @@
         )
         norm_tile(2, tile, before)
     low_grad = r.low_grad
-    gather.finish()
+    gather.finish(range(len(early), gather.last + 1))
 
     grad_rows, grad_columns = r.grad_rows, r.grad_columns
 
@@ -1435,8 +1439,8 @@
             pltpu.VMEM((max(high - low for low, high in bands(rows, rows, 512)), TILE), F32)
             for _ in range(2)
         ],
-        shares=[pltpu.VMEM((rows, TILE), BF16) for _ in range(2)],
-        score_grads=[pltpu.VMEM((rows, TILE), BF16) for _ in range(2)],
+        shares=[pltpu.VMEM((TILE, rows), BF16) for _ in range(2)],
+        score_grads=[pltpu.VMEM((TILE, rows), BF16) for _ in range(2)],
         in_tall=arrivals((tall_rows, D)),
         in_up=arrivals((wide_rows, FF)),
         in_mid=arrivals((wide_rows, 5 * D)),

time: 146 us -> 143 us (0.979)
  Pallas kernels: 142 us -> 140 us
    pallas_call x1, Pallas kernels: 138 us -> 135 us  [fused_body(): pl.pallas_call(kernel, out_shape=output_leaves, in_specs=spec, out_specs=...]
where the time goes in v4:
time: 143 us; the launch traced here: 140 us
  Pallas kernels  140 us (98%)
    pallas_call x1, Pallas kernels, fused_body(): pl.pallas_call(kernel, out_shape=output_leaves, in_specs=spec, out_specs=...  135 us
    pallas_call x1, Pallas kernels, fused_body(): pl.pallas_call(finish_kernel, out_shape=list(shapes.values()) + [jax.Shap...  4.32 us

profile of v4, /device:TPU:0, one launch (start us, length us, event | category | flops | bytes accessed | tf_op | source)
XLA Modules:
  0.0 140.4 jit_solution(18167499343621022063)
XLA Ops:
  0.6 135.2 %shard_map.178 = (bf16[1024,512]{1,0:T(8,128)(2,1)}, f32[1024,512]{1,0:T(8,128)}, f32[512,512]{1,0:T(8,128)}, f32[16,6144]{1,0:T(8,128)}, f32[96,512]{1,0:T(8,128)}, /*index=5*/f32[16,128]{1,0:T(8,128)}) custom-call(s32[1,6]{1,0:T(1,128)} %refs_0_.1, s32[1,6]{1,0:T(1,128)} %refs_1_.1, bf16[1024,512]{1,0:T(8,128)(2,1)} %refs_2_.1, bf16[512,512]{1,0:T(8,128)(2,1)} %refs_3_.1, ...), custom_call_target="tpu_custom_call" | custom-call | tf_op jit(solution)/shard_map/pallas_call | solution.py:1467
  135.9 4.3 %shard_map.179 = (bf16[1024,512]{1,0:T(8,128)(2,1)}, f32[1024,512]{1,0:T(8,128)}, f32[512,512]{1,0:T(8,128)}, f32[16,6144]{1,0:T(8,128)}, f32[96,512]{1,0:T(8,12...) custom-call(bf16[1024,512]{1,0:T(8,128)(2,1)} %get-tuple-element.15.refs_0_, ...), custom_call_target="tpu_custom_call" | custom-call | tf_op jit(solution)/shard_map/pallas_call | solution.py:1480
